TPU v7x, 32 devices: a whole 2x2x4 slice. The times are simulated.
32 devices in a mesh: sweep: 2 (over core), leaf: 16 (over z, y, x).
Axes of the slice: x: 2, y: 2, z: 4, core: 2. Of those that a mesh axis runs over, the one named last changes fastest.
Arguments:
- sources: bfloat16 [2, 16, 128, 384], P('sweep', 'leaf'), may hold values from -6 to 6
- solve_tiles: bfloat16 [2, 16, 384, 384], P('sweep', 'leaf'), may hold values from -0.3125 to 0.3125
- self_merge: bfloat16 [2, 16, 4, 384, 384], P('sweep', 'leaf'), may hold values from -0.21875 to 0.21875
- partner_merge: bfloat16 [2, 16, 4, 384, 384], P('sweep', 'leaf'), may hold values from -0.21875 to 0.21875
- coupling: bfloat16 [2, 16, 384, 384], P('sweep', 'leaf'), may hold values from -0.3125 to 0.3125
- front_map: int32 [2, 16, 4, 384], P('sweep', 'leaf'), may hold values from 0 to 383, each once within a row
Outputs:
- fronts: bfloat16 [2, 16, 128, 384], P('sweep', 'leaf')
Inputs may be any that keep to these rules, and one draw needn't show every extreme that they name: Each row front_map[s, l, j, :] is a permutation of 0 to 383.
All inputs are finite; a program needn't handle non-finite values.
Results may differ from a plain program's by a relative error of at most 0.039.
Values may be sent and summed in bfloat16 or wider, within the bound.
No kernel may reach another device: no remote copies, remote signals or barrier semaphores. Data moves between devices by JAX's collectives and lax.ppermute only.
A program may use at most 64 MiB of HBM per device.

v0:
```python
import jax
import jax.numpy as jnp
from jax import lax
from jax.experimental import pallas as pl
from jax.experimental.pallas import tpu as pltpu
from jax.sharding import PartitionSpec as P

BF = jnp.bfloat16
F32 = jnp.float32
MIB = 2**20
HINT = 10**8

HBM = pl.BlockSpec(memory_space=pltpu.HBM)
VMEM = pl.BlockSpec(memory_space=pltpu.VMEM)


def mm(left, right):
    return jnp.dot(left, right, preferred_element_type=F32)


def in_hbm(value):
    return pltpu.with_memory_space_constraint(value, pltpu.HBM)


def cost(flops, moved):
    return pl.CostEstimate(flops=flops, bytes_accessed=moved, transcendentals=0)


def side():
    return lax.rem(lax.axis_index("sweep"), 2)


def call(kernel, outs, args, flops, limit=4, **more):
    moved = sum(a.size * a.dtype.itemsize for a in args) + sum(o.size * 4 for o in outs)
    return pl.pallas_call(
        kernel,
        out_shape=tuple(pltpu.VMEM(o.shape, o.dtype) for o in outs),
        in_specs=[VMEM] * len(args),
        out_specs=(VMEM,) * len(outs),
        compiler_params=pltpu.CompilerParams(vmem_limit_bytes=limit * MIB),
        cost_estimate=cost(flops, moved),
        **more,
    )(*args)


def load_kernel(rows_hbm, solve_hbm, out_ref, rows_ref, solve_ref, sems):
    copies = [
        pltpu.make_async_copy(rows_hbm, rows_ref, sems.at[0]),
        pltpu.make_async_copy(solve_hbm, solve_ref, sems.at[1]),
    ]
    for copy in copies:
        copy.start()
    for copy in copies:
        copy.wait()
    out_ref[...] = mm(rows_ref[...], solve_ref[...]).astype(BF)


def load(rows, solve):
    return pl.pallas_call(
        load_kernel,
        out_shape=pltpu.VMEM(rows.shape, BF),
        in_specs=[HBM, HBM],
        out_specs=VMEM,
        scratch_shapes=[
            pltpu.VMEM(rows.shape, BF),
            pltpu.VMEM(solve.shape, BF),
            pltpu.SemaphoreType.DMA((2,)),
        ],
        compiler_params=pltpu.CompilerParams(vmem_limit_bytes=2 * MIB),
        cost_estimate=cost(2 * rows.size * solve.shape[1], 4 * rows.size + 2 * solve.size),
    )(in_hbm(rows), in_hbm(solve))


def prepare_kernel(levels, single, link, own_hbm, partner_hbm, map_hbm, *refs):
    number = len(levels)
    width = own_hbm.shape[1]
    link_hbm, refs = refs[: 2 * link], refs[2 * link :]
    outs, refs = refs[:number], refs[number:]
    singles, refs = refs[: 2 * single], refs[2 * single :]
    products, (partner_ref, map_ref, link_ref, sems, map_sem) = refs[:link], refs[link:]
    map_copy = pltpu.make_async_copy(map_hbm, map_ref, map_sem)
    map_copy.start()
    copies = []
    for k, j in enumerate(levels):
        pair = (
            pltpu.make_async_copy(partner_hbm.at[j], partner_ref.at[k], sems.at[2 * k]),
            pltpu.make_async_copy(own_hbm.at[j], outs[k].at[0], sems.at[2 * k + 1]),
        )
        for copy in pair:
            copy.start()
        copies.append(pair)
    extra = []
    if single:
        extra.append((own_hbm.at[levels[0]], singles[0]))
    for k, source in enumerate(link_hbm):
        extra.append((source, link_ref.at[k]))
    extra = [
        pltpu.make_async_copy(source, target, sems.at[2 * number + k])
        for k, (source, target) in enumerate(extra)
    ]
    for copy in extra:
        copy.start()
    map_copy.wait()
    rows = lax.broadcasted_iota(jnp.int32, (width, width), 0)
    for k, j in enumerate(levels):
        copies[k][0].wait()
        hot = (rows == map_ref[j : j + 1, :]).astype(BF)
        folded = mm(hot, partner_ref[k]).astype(BF)
        outs[k][1] = folded
        if single and k == 0:
            singles[1][...] = folded
    for copy in extra:
        copy.wait()
    if link:
        products[0][...] = mm(link_ref[0], link_ref[1]).astype(BF)
    for pair in copies:
        pair[1].wait()


def prepare(own, partner, index_map, levels, single=0, link=()):
    width = own.shape[1]
    number = len(levels)
    more = len(link) // 2
    outs = pl.pallas_call(
        lambda *refs: prepare_kernel(levels, single, more, *refs),
        out_shape=(pltpu.VMEM((2, width, width), BF),) * number
        + (pltpu.VMEM((width, width), BF),) * (2 * single + more),
        in_specs=[HBM] * (3 + len(link)),
        out_specs=(VMEM,) * (number + 2 * single + more),
        scratch_shapes=[
            pltpu.VMEM((number, width, width), BF),
            pltpu.VMEM(index_map.shape, jnp.int32),
            pltpu.VMEM((2, width, width), BF),
            pltpu.SemaphoreType.DMA((2 * number + 2,)),
            pltpu.SemaphoreType.DMA,
        ],
        compiler_params=pltpu.CompilerParams(vmem_limit_bytes=8 * MIB),
        cost_estimate=cost(2 * number * width**3, 8 * number * width**2),
    )(*(in_hbm(value) for value in (own, partner, index_map, *link)))
    return list(outs[:number]), list(outs[number:])


def level(which, rows, partner, table):
    def kernel(rows_ref, partner_ref, table_ref, out_ref):
        @pl.when(side() == which)
        def _():
            total = mm(rows_ref[...], table_ref[0]) + mm(partner_ref[...], table_ref[1])
            out_ref[...] = total.astype(BF)

    out = jax.ShapeDtypeStruct(rows.shape, BF)
    return call(kernel, [out], [rows, partner, table], HINT)[0]


def both_parts(which, rows, partner, table, start, count):
    def kernel(rows_ref, partner_ref, table_ref, out_ref):
        @pl.when(side() == which)
        def _():
            block = slice(start, start + count)
            total = mm(rows_ref[block], table_ref[0]) + mm(partner_ref[block], table_ref[1])
            out_ref[...] = total.astype(BF)

    out = jax.ShapeDtypeStruct((count, rows.shape[1]), BF)
    return call(kernel, [out], [rows, partner, table], HINT)[0]


def pass_on(which, front, x, link, start):
    count = front.shape[0]

    def kernel(front_ref, x_ref, link_ref, out_ref):
        @pl.when(side() == which)
        def _():
            known = x_ref[start : start + count].astype(F32)
            out_ref[...] = (known + mm(front_ref[...], link_ref[...])).astype(BF)

    return call(kernel, [jax.ShapeDtypeStruct(front.shape, BF)], [front, x, link], HINT)[0]


def write_kernel(which, first_ref, second_ref, out_ref, sems):
    half = first_ref.shape[0]

    @pl.when(side() == which)
    def _():
        copies = [
            pltpu.make_async_copy(first_ref, out_ref.at[pl.ds(0, half)], sems.at[0]),
            pltpu.make_async_copy(second_ref, out_ref.at[pl.ds(half, half)], sems.at[1]),
        ]
        for copy in copies:
            copy.start()
        for copy in copies:
            copy.wait()


def write_first(which, blocks):
    half, width = blocks[0].shape
    return pl.pallas_call(
        lambda first, second, out, sems: write_kernel(which, first, second, out, sems),
        out_shape=pltpu.HBM((2 * half, width), BF),
        in_specs=[VMEM, VMEM],
        out_specs=HBM,
        scratch_shapes=[pltpu.SemaphoreType.DMA((2,))],
        compiler_params=pltpu.CompilerParams(vmem_limit_bytes=2 * MIB),
        cost_estimate=cost(0, 8 * blocks[0].size),
    )(*blocks)


def write_rest(which, out, blocks):
    return pl.pallas_call(
        lambda first, second, _, out, sems: write_kernel(which, first, second, out, sems),
        out_shape=pltpu.HBM(out.shape, BF),
        in_specs=[VMEM, VMEM, HBM],
        out_specs=HBM,
        scratch_shapes=[pltpu.SemaphoreType.DMA((2,))],
        input_output_aliases={2: 0},
        compiler_params=pltpu.CompilerParams(vmem_limit_bytes=2 * MIB),
        cost_estimate=cost(0, 8 * blocks[0].size),
    )(*blocks, out)


def permute(value, target):
    sections, leaves = lax.axis_size("sweep"), lax.axis_size("leaf")
    pairs = []
    for s in range(sections):
        for l in range(leaves):
            to = target(s, l)
            if to is not None:
                pairs.append((s * leaves + l, to[0] * leaves + to[1]))
    return lax.ppermute(value, ("sweep", "leaf"), pairs)


def swap(value, bit, row):
    def target(s, l):
        ring = 2 if (l ^ l >> 1) & 1 else 1
        return s, l ^ (bit if s == row else ring)

    return permute(value, target)


def cross(value, bit=0):
    return permute(value, lambda s, l: (s ^ 1, l ^ bit))


def behind(rows, *values):
    rows, *values = lax.optimization_barrier((rows, *values))
    return rows, values


def paired(sources, solve_tiles, self_merge, partner_merge, coupling, front_map):
    solve = solve_tiles[0, 0]
    sections = lax.axis_size("sweep")
    count = self_merge.shape[2]

    x = load(sources[0, 0], solve)
    half = x.shape[0] // 2
    rows, raw = behind(x, self_merge, partner_merge, front_map, coupling)
    own = prepare(*(v[0, 0] for v in raw[:3]), [0, 1])[0]
    other = [None] * count
    own_link = None
    front = None
    even, odd = [], []
    back = out = None
    for section in range(sections):
        if section % 2 == 0:
            if section > 0:
                turn = {section - 1: section, section: section - 1}
                front = [permute(part, lambda s, l: (turn.get(s, s), l)) for part in front]
                rows = [pass_on(0, part, x, own_link, k * half) for k, part in enumerate(front)]
                rows = jnp.concatenate(rows)
            rows = both_parts(0, rows, swap(rows, 1, section), own[0], 0, 2 * half)
            if section == 0:
                rows, (table,) = behind(rows, own[1])
                other[1] = cross(table)
            came = cross(rows)
            partner = cross(rows, 2)
            if section == 0:
                _, raw = behind(rows, *raw)
                more, (own_link,) = prepare(
                    *(v[0, 0] for v in raw[:3]),
                    list(range(2, count)),
                    link=(raw[3][0, 0], solve),
                )
                own += more
            front = [both_parts(1, came, partner, other[1], k * half, half) for k in range(2)]
            first, tables, row = 2, other, section + 1
        else:
            front = [pass_on(1, part, x, own_link, k * half) for k, part in enumerate(front)]
            first, tables, row = 0, own, section
        for j in range(first, count):
            if section == 0 and j == 2:
                _, late = behind(front[0], *own[2:])
                other[2:] = [cross(table) for table in late]
            partners = [swap(part, 2**j, row) for part in front]
            if section % 2 and j == 1:
                _, back = behind(front[0], *back)
                back = [cross(part) for part in back]
            if section % 2 and j == 2:
                front[1], back = behind(front[1], *back)
                if sections == 2:
                    out = write_first(0, back)
                    front[1], (out,) = behind(front[1], out)
            front = [level(1, part, came, tables[j]) for part, came in zip(front, partners)]
        if section % 2 == 0:
            back = front
        elif section == 1:
            even, odd = back, front
        else:
            chosen = lax.axis_index("sweep") // 2 == section // 2
            even = [jnp.where(chosen, new, old) for new, old in zip(back, even)]
            odd = [jnp.where(chosen, new, old) for new, old in zip(front, odd)]
    if out is None:
        out = write_first(0, even)
    return write_rest(1, out, odd)[None, None]


def single(sources, solve_tiles, self_merge, partner_merge, coupling, front_map):
    rows, solve, link = sources[0, 0], solve_tiles[0, 0], coupling[0, 0]
    sections = lax.axis_size("sweep")
    front = jnp.zeros_like(rows)
    for section in range(sections):
        front = permute(front, lambda s, l: ((s + 1) % sections, l))
        front = jnp.where(lax.axis_index("sweep") == 0, jnp.zeros_like(front), front)
        x = mm((rows.astype(F32) + mm(front, link)).astype(BF), solve).astype(BF)
        for j in range(self_merge.shape[2]):
            mapped = jnp.take(swap(x, 2**j), front_map[0, 0, j], axis=1)
            x = (mm(x, self_merge[0, 0, j]) + mm(mapped, partner_merge[0, 0, j])).astype(BF)
        front = x
    return front[None, None]


def solution(mesh):
    spec = P("sweep", "leaf")
    return jax.shard_map(
        paired if mesh.shape["sweep"] % 2 == 0 else single,
        mesh=mesh,
        in_specs=(spec,) * 6,
        out_specs=spec,
        check_vma=False,
    )
```

profile of v0, /device:TPU:0, one launch (start us, length us, event | category | flops | bytes accessed | tf_op | source)
XLA Modules:
  0.0 39.2 jit_solution(14472731729511617458)
XLA Ops:
  0.0 1.2 %shard_map.64.rows_ref.x_ref = bf16[128,384]{1,0:T(8,128)(2,1)S(1)} custom-call(bf16[128,384]{1,0:T(8,128)(2,1)} %bitcast.17, bf16[384,384]{1,0:T(8,128)(2,1)} %bitcast.14), custom_call_target="tpu_custom_call" | custom-call | flops 37748736 | bytes 491520 | tf_op jit(solution)/shard_map/pallas_call | solution.py:59
  1.3 3.0 %collective-permute-start = (bf16[128,384]{1,0:T(8,128)(2,1)S(1)}, bf16[128,384]{1,0:T(8,128)(2,1)S(1)}, u32[]{:S(2)}, u32[]{:S(2)}) collective-permute-start(bf16[128,384]{1,0:T(8,128)(2,1)S(1)} %shard_map.64.rows_ref.x_ref), channel_id=1, source_target_pairs={{0,1},{1,0},{2,3},{3,2},{4,5},{5,4},{6,7},{7,6},{8,9},{9,8},{10,11... | collective-permute-start | bytes 294920 | tf_op jit(solution)/shard_map/ppermute | solution.py:227
  4.2 1.8 %shard_map.65 = (bf16[2,384,384]{2,1,0:T(8,128)(2,1)S(1)}, bf16[2,384,384]{2,1,0:T(8,128)(2,1)S(1)}) custom-call(bf16[4,384,384]{2,1,0:T(8,128)(2,1)} %bitcast.10, bf16[4,384,384]{2,1,0:T(8,128)(2,1)} %bitcast.12, s32[4,384]{1,0:T(4,128)} %bitcast.18), custom_call_target="tpu_custom_call" | custom-call | flops 226492416 | bytes 2359296 | tf_op jit(solution)/shard_map/pallas_call | solution.py:124
  6.1 0.8 %collective-permute-done.partner_ref = bf16[128,384]{1,0:T(8,128)(2,1)S(1)} collective-permute-done((bf16[128,384]{1,0:T(8,128)(2,1)S(1)}, bf16[128,384]{1,0:T(8,128)(2,1)S(1)}, u32[]{:S(2)}, u32[]{:S(2)}) %collective-permute-start) | collective-permute-done | bytes 98336 | tf_op jit(solution)/shard_map/ppermute | solution.py:227
  7.2 2.2 %collective-permute-start.2 = (bf16[128,384]{1,0:T(8,128)(2,1)S(1)}, bf16[128,384]{1,0:T(8,128)(2,1)S(1)}, u32[]{:S(2)}, u32[]{:S(2)}) collective-permute-start(bf16[128,384]{1,0:T(8,128)(2,1)S(1)} %shard_map.66), channel_id=1, source_target_pairs={{0,18},{1,19},{2,16},{3,17},{4,22},{5,23},{6,20},{7,21},{8,26},{9,... | collective-permute-start | bytes 294920 | tf_op jit(solution)/shard_map/ppermute | solution.py:227
  9.4 2.4 %shard_map.68 = (bf16[2,384,384]{2,1,0:T(8,128)(2,1)S(1)}, bf16[2,384,384]{2,1,0:T(8,128)(2,1)S(1)}, bf16[384,384]{1,0:T(8,128)(2,1)S(1)}) custom-call(bf16[4,384,384]{2,1,0:T(8,128)(2,1)} %bitcast.11, bf16[4,384,384]{2,1,0:T(8,128)(2,1)} %bitcast.13, s32[4,384]{1,0:T(4,128)} %bitcast.19, bf16[384,384]{1,0:T(8,128)(2,1)} %bitcast.16, bf16[384,384]{1,0:T(8,128)(2,1)} %bitcast.15), custom_call_target="tpu_custom_call" | custom-call | flops 226492416 | bytes 2359296 | tf_op jit(solution)/shard_map/pallas_call | solution.py:124
  13.0 1.6 %collective-permute-start.4 = (bf16[64,384]{1,0:T(8,128)(2,1)S(1)}, bf16[64,384]{1,0:T(8,128)(2,1)S(1)}, u32[]{:S(2)}, u32[]{:S(2)}) collective-permute-start(bf16[64,384]{1,0:T(8,128)(2,1)S(1)} %shard_map.67.rows_ref), channel_id=1, source_target_pairs={{0,1},{1,3},{2,0},{3,2},{4,5},{5,7},{6,4},{7,6},{8,9},{9,11},{10,8... | collective-permute-start | bytes 147464 | tf_op jit(solution)/shard_map/ppermute | solution.py:227
  14.6 1.5 %collective-permute-start.12 = (bf16[64,384]{1,0:T(8,128)(2,1)S(1)}, bf16[64,384]{1,0:T(8,128)(2,1)S(1)}, u32[]{:S(2)}, u32[]{:S(2)}) collective-permute-start(bf16[64,384]{1,0:T(8,128)(2,1)S(1)} %shard_map.76.rows_ref), channel_id=1, source_target_pairs={{0,1},{1,3},{2,0},{3,2},{4,5},{5,7},{6,4},{7,6},{8,9},{9,11},{10,8... | collective-permute-start | bytes 147464 | tf_op jit(solution)/shard_map/ppermute | solution.py:227
  16.1 1.0 %collective-permute-done.4.partner_ref = bf16[64,384]{1,0:T(8,128)(2,1)S(1)} collective-permute-done((bf16[64,384]{1,0:T(8,128)(2,1)S(1)}, bf16[64,384]{1,0:T(8,128)(2,1)S(1)}, u32[]{:S(2)}, u32[]{:S(2)}) %collective-permute-start.4) | collective-permute-done | bytes 49184 | tf_op jit(solution)/shard_map/ppermute | solution.py:227
  17.1 1.6 %collective-permute-start.6 = (bf16[64,384]{1,0:T(8,128)(2,1)S(1)}, bf16[64,384]{1,0:T(8,128)(2,1)S(1)}, u32[]{:S(2)}, u32[]{:S(2)}) collective-permute-start(bf16[64,384]{1,0:T(8,128)(2,1)S(1)} %shard_map.69.rows_ref), channel_id=1, source_target_pairs={{0,1},{1,3},{2,0},{3,2},{4,5},{5,7},{6,4},{7,6},{8,9},{9,11},{10,8... | collective-permute-start | bytes 147464 | tf_op jit(solution)/shard_map/ppermute | solution.py:227
  18.7 1.5 %collective-permute-start.13 = (bf16[64,384]{1,0:T(8,128)(2,1)S(1)}, bf16[64,384]{1,0:T(8,128)(2,1)S(1)}, u32[]{:S(2)}, u32[]{:S(2)}) collective-permute-start(bf16[64,384]{1,0:T(8,128)(2,1)S(1)} %shard_map.77.rows_ref), channel_id=1, source_target_pairs={{0,1},{1,3},{2,0},{3,2},{4,5},{5,7},{6,4},{7,6},{8,9},{9,11},{10,8... | collective-permute-start | bytes 147464 | tf_op jit(solution)/shard_map/ppermute | solution.py:227
  20.2 1.0 %collective-permute-done.6.partner_ref = bf16[64,384]{1,0:T(8,128)(2,1)S(1)} collective-permute-done((bf16[64,384]{1,0:T(8,128)(2,1)S(1)}, bf16[64,384]{1,0:T(8,128)(2,1)S(1)}, u32[]{:S(2)}, u32[]{:S(2)}) %collective-permute-start.6) | collective-permute-done | bytes 49184 | tf_op jit(solution)/shard_map/ppermute | solution.py:227
  21.2 1.6 %collective-permute-start.8 = (bf16[64,384]{1,0:T(8,128)(2,1)S(1)}, bf16[64,384]{1,0:T(8,128)(2,1)S(1)}, u32[]{:S(2)}, u32[]{:S(2)}) collective-permute-start(bf16[64,384]{1,0:T(8,128)(2,1)S(1)} %shard_map.71.rows_ref), channel_id=1, source_target_pairs={{0,1},{1,3},{2,0},{3,2},{4,5},{5,7},{6,4},{7,6},{8,9},{9,11},{10,8... | collective-permute-start | bytes 147464 | tf_op jit(solution)/shard_map/ppermute | solution.py:227
  22.8 1.5 %collective-permute-start.14 = (bf16[64,384]{1,0:T(8,128)(2,1)S(1)}, bf16[64,384]{1,0:T(8,128)(2,1)S(1)}, u32[]{:S(2)}, u32[]{:S(2)}) collective-permute-start(bf16[64,384]{1,0:T(8,128)(2,1)S(1)} %shard_map.79.rows_ref), channel_id=1, source_target_pairs={{0,1},{1,3},{2,0},{3,2},{4,5},{5,7},{6,4},{7,6},{8,9},{9,11},{10,8... | collective-permute-start | bytes 147464 | tf_op jit(solution)/shard_map/ppermute | solution.py:227
  24.3 1.0 %collective-permute-done.8.partner_ref = bf16[64,384]{1,0:T(8,128)(2,1)S(1)} collective-permute-done((bf16[64,384]{1,0:T(8,128)(2,1)S(1)}, bf16[64,384]{1,0:T(8,128)(2,1)S(1)}, u32[]{:S(2)}, u32[]{:S(2)}) %collective-permute-start.8) | collective-permute-done | bytes 49184 | tf_op jit(solution)/shard_map/ppermute | solution.py:227
  25.3 1.6 %collective-permute-start.9 = (bf16[64,384]{1,0:T(8,128)(2,1)S(1)}, bf16[64,384]{1,0:T(8,128)(2,1)S(1)}, u32[]{:S(2)}, u32[]{:S(2)}) collective-permute-start(bf16[64,384]{1,0:T(8,128)(2,1)S(1)} %shard_map.72.rows_ref), channel_id=1, source_target_pairs={{0,1},{1,3},{2,0},{3,2},{4,5},{5,7},{6,4},{7,6},{8,9},{9,11},{10,8... | collective-permute-start | bytes 147464 | tf_op jit(solution)/shard_map/ppermute | solution.py:227
  26.9 1.9 %collective-permute-start.15 = (bf16[64,384]{1,0:T(8,128)(2,1)S(1)}, bf16[64,384]{1,0:T(8,128)(2,1)S(1)}, u32[]{:S(2)}, u32[]{:S(2)}) collective-permute-start(bf16[64,384]{1,0:T(8,128)(2,1)S(1)} %shard_map.80.rows_ref), channel_id=1, source_target_pairs={{0,1},{1,3},{2,0},{3,2},{4,5},{5,7},{6,4},{7,6},{8,9},{9,11},{10,8... | collective-permute-start | bytes 147464 | tf_op jit(solution)/shard_map/ppermute | solution.py:227
  29.4 1.6 %collective-permute-start.10 = (bf16[64,384]{1,0:T(8,128)(2,1)S(1)}, bf16[64,384]{1,0:T(8,128)(2,1)S(1)}, u32[]{:S(2)}, u32[]{:S(2)}) collective-permute-start(bf16[64,384]{1,0:T(8,128)(2,1)S(1)} %shard_map.73.rows_ref), channel_id=1, source_target_pairs={{0,1},{1,3},{2,0},{3,2},{4,5},{5,7},{6,4},{7,6},{8,9},{9,11},{10,8... | collective-permute-start | bytes 147464 | tf_op jit(solution)/shard_map/ppermute | solution.py:227
  31.0 1.9 %collective-permute-start.18 = (bf16[64,384]{1,0:T(8,128)(2,1)S(1)}, bf16[64,384]{1,0:T(8,128)(2,1)S(1)}, u32[]{:S(2)}, u32[]{:S(2)}) collective-permute-start(bf16[64,384]{1,0:T(8,128)(2,1)S(1)} %shard_map.81.rows_ref), channel_id=1, source_target_pairs={{0,1},{1,3},{2,0},{3,2},{4,5},{5,7},{6,4},{7,6},{8,9},{9,11},{10,8... | collective-permute-start | bytes 147464 | tf_op jit(solution)/shard_map/ppermute | solution.py:227
  32.9 0.7 %shard_map.82._ = bf16[128,384]{1,0:T(8,128)(2,1)} custom-call(bf16[64,384]{1,0:T(8,128)(2,1)S(1)} %collective-permute-done.16.first, bf16[64,384]{1,0:T(8,128)(2,1)S(1)} %collective-permute-done.17.second), custom_call_target="tpu_custom_call" | custom-call | bytes 196608 | tf_op jit(solution)/shard_map/pallas_call | solution.py:195
  33.6 1.4 %collective-permute-start.11 = (bf16[64,384]{1,0:T(8,128)(2,1)S(1)}, bf16[64,384]{1,0:T(8,128)(2,1)S(1)}, u32[]{:S(2)}, u32[]{:S(2)}) collective-permute-start(bf16[64,384]{1,0:T(8,128)(2,1)S(1)} %shard_map.74.rows_ref), channel_id=1, source_target_pairs={{0,1},{1,3},{2,0},{3,2},{4,5},{5,7},{6,4},{7,6},{8,9},{9,11},{10,8... | collective-permute-start | bytes 147464 | tf_op jit(solution)/shard_map/ppermute | solution.py:227
  35.1 1.9 %collective-permute-start.19 = (bf16[64,384]{1,0:T(8,128)(2,1)S(1)}, bf16[64,384]{1,0:T(8,128)(2,1)S(1)}, u32[]{:S(2)}, u32[]{:S(2)}) collective-permute-start(bf16[64,384]{1,0:T(8,128)(2,1)S(1)} %shard_map.83.rows_ref), channel_id=1, source_target_pairs={{0,1},{1,3},{2,0},{3,2},{4,5},{5,7},{6,4},{7,6},{8,9},{9,11},{10,8... | collective-permute-start | bytes 147464 | tf_op jit(solution)/shard_map/ppermute | solution.py:227
  37.0 0.8 %collective-permute-done.11.partner_ref = bf16[64,384]{1,0:T(8,128)(2,1)S(1)} collective-permute-done((bf16[64,384]{1,0:T(8,128)(2,1)S(1)}, bf16[64,384]{1,0:T(8,128)(2,1)S(1)}, u32[]{:S(2)}, u32[]{:S(2)}) %collective-permute-start.11) | collective-permute-done | bytes 49184 | tf_op jit(solution)/shard_map/ppermute | solution.py:227
  37.8 1.4 %collective-permute-done.19.partner_ref = bf16[64,384]{1,0:T(8,128)(2,1)S(1)} collective-permute-done((bf16[64,384]{1,0:T(8,128)(2,1)S(1)}, bf16[64,384]{1,0:T(8,128)(2,1)S(1)}, u32[]{:S(2)}, u32[]{:S(2)}) %collective-permute-start.19) | collective-permute-done | bytes 49184 | tf_op jit(solution)/shard_map/ppermute | solution.py:227
  (38 shorter events, 2.2 us)
Async XLA Ops:
  1.3 5.6 %collective-permute-start = (bf16[128,384]{1,0:T(8,128)(2,1)S(1)}, bf16[128,384]{1,0:T(8,128)(2,1)S(1)}, u32[]{:S(2)}, u32[]{:S(2)}) collective-permute-start(bf16[128,384]{1,0:T(8,128)(2,1)S(1)} %shard_map.64.rows_ref.x_ref), channel_id=1, source_target_pairs={{0,1},{1,0},{2,3},{3,2},{4,5},{5,4},{6,7},{7,6},{8,9},{9,8},{10,11... | collective-permute-start | bytes 294920 | tf_op jit(solution)/shard_map/ppermute | solution.py:227
  7.1 5.3 %collective-permute-start.3 = (bf16[2,384,384]{2,1,0:T(8,128)(2,1)S(1)}, bf16[2,384,384]{2,1,0:T(8,128)(2,1)S(1)}, u32[]{:S(2)}, u32[]{:S(2)}) collective-permute-start(bf16[2,384,384]{2,1,0:T(8,128)(2,1)S(1)} %get-tuple-element.37.table_ref), channel_id=1, source_target_pairs={{0,16},{1,17},{2,18},{3,19},{4,20},{5,21},{6,22},{7,23},{8,24},{9,... | collective-permute-start | bytes 1769480 | tf_op jit(solution)/shard_map/ppermute | solution.py:227
  7.2 5.2 %collective-permute-start.2 = (bf16[128,384]{1,0:T(8,128)(2,1)S(1)}, bf16[128,384]{1,0:T(8,128)(2,1)S(1)}, u32[]{:S(2)}, u32[]{:S(2)}) collective-permute-start(bf16[128,384]{1,0:T(8,128)(2,1)S(1)} %shard_map.66), channel_id=1, source_target_pairs={{0,18},{1,19},{2,16},{3,17},{4,22},{5,23},{6,20},{7,21},{8,26},{9,... | collective-permute-start | bytes 294920 | tf_op jit(solution)/shard_map/ppermute | solution.py:227
  9.4 3.1 %collective-permute-start.1 = (bf16[128,384]{1,0:T(8,128)(2,1)S(1)}, bf16[128,384]{1,0:T(8,128)(2,1)S(1)}, u32[]{:S(2)}, u32[]{:S(2)}) collective-permute-start(bf16[128,384]{1,0:T(8,128)(2,1)S(1)} %shard_map.66), channel_id=1, source_target_pairs={{0,16},{1,17},{2,18},{3,19},{4,20},{5,21},{6,22},{7,23},{8,24},{9,... | collective-permute-start | bytes 294920 | tf_op jit(solution)/shard_map/ppermute | solution.py:227
  12.4 4.7 %collective-permute-start.5 = (bf16[2,384,384]{2,1,0:T(8,128)(2,1)S(1)}, bf16[2,384,384]{2,1,0:T(8,128)(2,1)S(1)}, u32[]{:S(2)}, u32[]{:S(2)}) collective-permute-start(bf16[2,384,384]{2,1,0:T(8,128)(2,1)S(1)} %get-tuple-element.45.table_ref), channel_id=1, source_target_pairs={{0,16},{1,17},{2,18},{3,19},{4,20},{5,21},{6,22},{7,23},{8,24},{9,... | collective-permute-start | bytes 1769480 | tf_op jit(solution)/shard_map/ppermute | solution.py:227
  12.8 7.4 %collective-permute-start.7 = (bf16[2,384,384]{2,1,0:T(8,128)(2,1)S(1)}, bf16[2,384,384]{2,1,0:T(8,128)(2,1)S(1)}, u32[]{:S(2)}, u32[]{:S(2)}) collective-permute-start(bf16[2,384,384]{2,1,0:T(8,128)(2,1)S(1)} %get-tuple-element.46.table_ref), channel_id=1, source_target_pairs={{0,16},{1,17},{2,18},{3,19},{4,20},{5,21},{6,22},{7,23},{8,24},{9,... | collective-permute-start | bytes 1769480 | tf_op jit(solution)/shard_map/ppermute | solution.py:227
  13.0 4.1 %collective-permute-start.4 = (bf16[64,384]{1,0:T(8,128)(2,1)S(1)}, bf16[64,384]{1,0:T(8,128)(2,1)S(1)}, u32[]{:S(2)}, u32[]{:S(2)}) collective-permute-start(bf16[64,384]{1,0:T(8,128)(2,1)S(1)} %shard_map.67.rows_ref), channel_id=1, source_target_pairs={{0,1},{1,3},{2,0},{3,2},{4,5},{5,7},{6,4},{7,6},{8,9},{9,11},{10,8... | collective-permute-start | bytes 147464 | tf_op jit(solution)/shard_map/ppermute | solution.py:227
  14.6 4.1 %collective-permute-start.12 = (bf16[64,384]{1,0:T(8,128)(2,1)S(1)}, bf16[64,384]{1,0:T(8,128)(2,1)S(1)}, u32[]{:S(2)}, u32[]{:S(2)}) collective-permute-start(bf16[64,384]{1,0:T(8,128)(2,1)S(1)} %shard_map.76.rows_ref), channel_id=1, source_target_pairs={{0,1},{1,3},{2,0},{3,2},{4,5},{5,7},{6,4},{7,6},{8,9},{9,11},{10,8... | collective-permute-start | bytes 147464 | tf_op jit(solution)/shard_map/ppermute | solution.py:227
  17.1 4.1 %collective-permute-start.6 = (bf16[64,384]{1,0:T(8,128)(2,1)S(1)}, bf16[64,384]{1,0:T(8,128)(2,1)S(1)}, u32[]{:S(2)}, u32[]{:S(2)}) collective-permute-start(bf16[64,384]{1,0:T(8,128)(2,1)S(1)} %shard_map.69.rows_ref), channel_id=1, source_target_pairs={{0,1},{1,3},{2,0},{3,2},{4,5},{5,7},{6,4},{7,6},{8,9},{9,11},{10,8... | collective-permute-start | bytes 147464 | tf_op jit(solution)/shard_map/ppermute | solution.py:227
  18.7 4.1 %collective-permute-start.13 = (bf16[64,384]{1,0:T(8,128)(2,1)S(1)}, bf16[64,384]{1,0:T(8,128)(2,1)S(1)}, u32[]{:S(2)}, u32[]{:S(2)}) collective-permute-start(bf16[64,384]{1,0:T(8,128)(2,1)S(1)} %shard_map.77.rows_ref), channel_id=1, source_target_pairs={{0,1},{1,3},{2,0},{3,2},{4,5},{5,7},{6,4},{7,6},{8,9},{9,11},{10,8... | collective-permute-start | bytes 147464 | tf_op jit(solution)/shard_map/ppermute | solution.py:227
  21.2 4.1 %collective-permute-start.8 = (bf16[64,384]{1,0:T(8,128)(2,1)S(1)}, bf16[64,384]{1,0:T(8,128)(2,1)S(1)}, u32[]{:S(2)}, u32[]{:S(2)}) collective-permute-start(bf16[64,384]{1,0:T(8,128)(2,1)S(1)} %shard_map.71.rows_ref), channel_id=1, source_target_pairs={{0,1},{1,3},{2,0},{3,2},{4,5},{5,7},{6,4},{7,6},{8,9},{9,11},{10,8... | collective-permute-start | bytes 147464 | tf_op jit(solution)/shard_map/ppermute | solution.py:227
  22.8 4.1 %collective-permute-start.14 = (bf16[64,384]{1,0:T(8,128)(2,1)S(1)}, bf16[64,384]{1,0:T(8,128)(2,1)S(1)}, u32[]{:S(2)}, u32[]{:S(2)}) collective-permute-start(bf16[64,384]{1,0:T(8,128)(2,1)S(1)} %shard_map.79.rows_ref), channel_id=1, source_target_pairs={{0,1},{1,3},{2,0},{3,2},{4,5},{5,7},{6,4},{7,6},{8,9},{9,11},{10,8... | collective-permute-start | bytes 147464 | tf_op jit(solution)/shard_map/ppermute | solution.py:227
  25.3 4.1 %collective-permute-start.9 = (bf16[64,384]{1,0:T(8,128)(2,1)S(1)}, bf16[64,384]{1,0:T(8,128)(2,1)S(1)}, u32[]{:S(2)}, u32[]{:S(2)}) collective-permute-start(bf16[64,384]{1,0:T(8,128)(2,1)S(1)} %shard_map.72.rows_ref), channel_id=1, source_target_pairs={{0,1},{1,3},{2,0},{3,2},{4,5},{5,7},{6,4},{7,6},{8,9},{9,11},{10,8... | collective-permute-start | bytes 147464 | tf_op jit(solution)/shard_map/ppermute | solution.py:227
  26.9 4.1 %collective-permute-start.15 = (bf16[64,384]{1,0:T(8,128)(2,1)S(1)}, bf16[64,384]{1,0:T(8,128)(2,1)S(1)}, u32[]{:S(2)}, u32[]{:S(2)}) collective-permute-start(bf16[64,384]{1,0:T(8,128)(2,1)S(1)} %shard_map.80.rows_ref), channel_id=1, source_target_pairs={{0,1},{1,3},{2,0},{3,2},{4,5},{5,7},{6,4},{7,6},{8,9},{9,11},{10,8... | collective-permute-start | bytes 147464 | tf_op jit(solution)/shard_map/ppermute | solution.py:227
  28.8 4.1 %collective-permute-start.16 = (bf16[64,384]{1,0:T(8,128)(2,1)S(1)}, bf16[64,384]{1,0:T(8,128)(2,1)S(1)}, u32[]{:S(2)}, u32[]{:S(2)}) collective-permute-start(bf16[64,384]{1,0:T(8,128)(2,1)S(1)} %shard_map.70.front_ref), channel_id=1, source_target_pairs={{0,16},{1,17},{2,18},{3,19},{4,20},{5,21},{6,22},{7,23},{8,24},{9,... | collective-permute-start | bytes 147464 | tf_op jit(solution)/shard_map/ppermute | solution.py:227
  28.8 4.1 %collective-permute-start.17 = (bf16[64,384]{1,0:T(8,128)(2,1)S(1)}, bf16[64,384]{1,0:T(8,128)(2,1)S(1)}, u32[]{:S(2)}, u32[]{:S(2)}) collective-permute-start(bf16[64,384]{1,0:T(8,128)(2,1)S(1)} %shard_map.78.front_ref), channel_id=1, source_target_pairs={{0,16},{1,17},{2,18},{3,19},{4,20},{5,21},{6,22},{7,23},{8,24},{9,... | collective-permute-start | bytes 147464 | tf_op jit(solution)/shard_map/ppermute | solution.py:227
  29.4 4.2 %collective-permute-start.10 = (bf16[64,384]{1,0:T(8,128)(2,1)S(1)}, bf16[64,384]{1,0:T(8,128)(2,1)S(1)}, u32[]{:S(2)}, u32[]{:S(2)}) collective-permute-start(bf16[64,384]{1,0:T(8,128)(2,1)S(1)} %shard_map.73.rows_ref), channel_id=1, source_target_pairs={{0,1},{1,3},{2,0},{3,2},{4,5},{5,7},{6,4},{7,6},{8,9},{9,11},{10,8... | collective-permute-start | bytes 147464 | tf_op jit(solution)/shard_map/ppermute | solution.py:227
  31.0 4.1 %collective-permute-start.18 = (bf16[64,384]{1,0:T(8,128)(2,1)S(1)}, bf16[64,384]{1,0:T(8,128)(2,1)S(1)}, u32[]{:S(2)}, u32[]{:S(2)}) collective-permute-start(bf16[64,384]{1,0:T(8,128)(2,1)S(1)} %shard_map.81.rows_ref), channel_id=1, source_target_pairs={{0,1},{1,3},{2,0},{3,2},{4,5},{5,7},{6,4},{7,6},{8,9},{9,11},{10,8... | collective-permute-start | bytes 147464 | tf_op jit(solution)/shard_map/ppermute | solution.py:227
  33.6 4.1 %collective-permute-start.11 = (bf16[64,384]{1,0:T(8,128)(2,1)S(1)}, bf16[64,384]{1,0:T(8,128)(2,1)S(1)}, u32[]{:S(2)}, u32[]{:S(2)}) collective-permute-start(bf16[64,384]{1,0:T(8,128)(2,1)S(1)} %shard_map.74.rows_ref), channel_id=1, source_target_pairs={{0,1},{1,3},{2,0},{3,2},{4,5},{5,7},{6,4},{7,6},{8,9},{9,11},{10,8... | collective-permute-start | bytes 147464 | tf_op jit(solution)/shard_map/ppermute | solution.py:227
  35.1 4.1 %collective-permute-start.19 = (bf16[64,384]{1,0:T(8,128)(2,1)S(1)}, bf16[64,384]{1,0:T(8,128)(2,1)S(1)}, u32[]{:S(2)}, u32[]{:S(2)}) collective-permute-start(bf16[64,384]{1,0:T(8,128)(2,1)S(1)} %shard_map.83.rows_ref), channel_id=1, source_target_pairs={{0,1},{1,3},{2,0},{3,2},{4,5},{5,7},{6,4},{7,6},{8,9},{9,11},{10,8... | collective-permute-start | bytes 147464 | tf_op jit(solution)/shard_map/ppermute | solution.py:227
where the time goes:
time: 39.5 us; the launch traced here: 39.2 us
  starting transfers between devices  26.2 us (66%)
  waiting for transfers between devices  6.51 us (16%)
  Pallas kernels  6.4 us (16%)
    ppermute x20, starting transfers between devices, permute(): return lax.ppermute(value, ('sweep', 'leaf'), pairs)  26.2 us
    ppermute x20, waiting for transfers between devices, permute(): return lax.ppermute(value, ('sweep', 'leaf'), pairs)  6.51 us
    pallas_call x2, Pallas kernels, prepare(): pl.pallas_call(lambda *refs: prepare_kernel(levels, single, more, *refs),...  4.18 us
    pallas_call x1, Pallas kernels, load(): pl.pallas_call(load_kernel, out_shape=pltpu.VMEM(rows.shape, BF), in_spec...  1.24 us
  transfers between devices with their start and end apart: 20, of which 7 were waited for; matrix products, arithmetic and copies ran while one was open for 0% of the time, Pallas kernels for 12%

commit v1 on v0

--- a/solution.py
+++ b/solution.py
@@ -320,7 +320,8 @@
         front = jnp.where(lax.axis_index("sweep") == 0, jnp.zeros_like(front), front)
         x = mm((rows.astype(F32) + mm(front, link)).astype(BF), solve).astype(BF)
         for j in range(self_merge.shape[2]):
-            mapped = jnp.take(swap(x, 2**j), front_map[0, 0, j], axis=1)
+            other = permute(x, lambda s, l, bit=2**j: (s, l ^ bit))
+            mapped = jnp.take(other, front_map[0, 0, j], axis=1)
             x = (mm(x, self_merge[0, 0, j]) + mm(mapped, partner_merge[0, 0, j])).astype(BF)
         front = x
     return front[None, None]

time: 39.5 us -> 39.5 us (level)
  no operation moved by 1% of the time
where the time goes in v1:
time: 39.5 us; the launch traced here: 39.2 us
  starting transfers between devices  26.2 us (66%)
  waiting for transfers between devices  6.51 us (16%)
  Pallas kernels  6.4 us (16%)
    ppermute x20, starting transfers between devices, permute(): return lax.ppermute(value, ('sweep', 'leaf'), pairs)  26.2 us
    ppermute x20, waiting for transfers between devices, permute(): return lax.ppermute(value, ('sweep', 'leaf'), pairs)  6.51 us
    pallas_call x2, Pallas kernels, prepare(): pl.pallas_call(lambda *refs: prepare_kernel(levels, single, more, *refs),...  4.18 us
    pallas_call x1, Pallas kernels, load(): pl.pallas_call(load_kernel, out_shape=pltpu.VMEM(rows.shape, BF), in_spec...  1.24 us
  transfers between devices with their start and end apart: 20, of which 7 were waited for; matrix products, arithmetic and copies ran while one was open for 0% of the time, Pallas kernels for 12%

profile of v1, /device:TPU:0, one launch (start us, length us, event | category | flops | bytes accessed | tf_op | source)
XLA Modules:
  0.0 39.2 jit_solution(14472731729511617458)
XLA Ops:
  0.0 1.2 %shard_map.64.rows_ref.x_ref = bf16[128,384]{1,0:T(8,128)(2,1)S(1)} custom-call(bf16[128,384]{1,0:T(8,128)(2,1)} %bitcast.17, bf16[384,384]{1,0:T(8,128)(2,1)} %bitcast.14), custom_call_target="tpu_custom_call" | custom-call | flops 37748736 | bytes 491520 | tf_op jit(solution)/shard_map/pallas_call | solution.py:59
  1.3 3.0 %collective-permute-start = (bf16[128,384]{1,0:T(8,128)(2,1)S(1)}, bf16[128,384]{1,0:T(8,128)(2,1)S(1)}, u32[]{:S(2)}, u32[]{:S(2)}) collective-permute-start(bf16[128,384]{1,0:T(8,128)(2,1)S(1)} %shard_map.64.rows_ref.x_ref), channel_id=1, source_target_pairs={{0,1},{1,0},{2,3},{3,2},{4,5},{5,4},{6,7},{7,6},{8,9},{9,8},{10,11... | collective-permute-start | bytes 294920 | tf_op jit(solution)/shard_map/ppermute | solution.py:227
  4.2 1.8 %shard_map.65 = (bf16[2,384,384]{2,1,0:T(8,128)(2,1)S(1)}, bf16[2,384,384]{2,1,0:T(8,128)(2,1)S(1)}) custom-call(bf16[4,384,384]{2,1,0:T(8,128)(2,1)} %bitcast.10, bf16[4,384,384]{2,1,0:T(8,128)(2,1)} %bitcast.12, s32[4,384]{1,0:T(4,128)} %bitcast.18), custom_call_target="tpu_custom_call" | custom-call | flops 226492416 | bytes 2359296 | tf_op jit(solution)/shard_map/pallas_call | solution.py:124
  6.1 0.8 %collective-permute-done.partner_ref = bf16[128,384]{1,0:T(8,128)(2,1)S(1)} collective-permute-done((bf16[128,384]{1,0:T(8,128)(2,1)S(1)}, bf16[128,384]{1,0:T(8,128)(2,1)S(1)}, u32[]{:S(2)}, u32[]{:S(2)}) %collective-permute-start) | collective-permute-done | bytes 98336 | tf_op jit(solution)/shard_map/ppermute | solution.py:227
  7.2 2.2 %collective-permute-start.2 = (bf16[128,384]{1,0:T(8,128)(2,1)S(1)}, bf16[128,384]{1,0:T(8,128)(2,1)S(1)}, u32[]{:S(2)}, u32[]{:S(2)}) collective-permute-start(bf16[128,384]{1,0:T(8,128)(2,1)S(1)} %shard_map.66), channel_id=1, source_target_pairs={{0,18},{1,19},{2,16},{3,17},{4,22},{5,23},{6,20},{7,21},{8,26},{9,... | collective-permute-start | bytes 294920 | tf_op jit(solution)/shard_map/ppermute | solution.py:227
  9.4 2.4 %shard_map.68 = (bf16[2,384,384]{2,1,0:T(8,128)(2,1)S(1)}, bf16[2,384,384]{2,1,0:T(8,128)(2,1)S(1)}, bf16[384,384]{1,0:T(8,128)(2,1)S(1)}) custom-call(bf16[4,384,384]{2,1,0:T(8,128)(2,1)} %bitcast.11, bf16[4,384,384]{2,1,0:T(8,128)(2,1)} %bitcast.13, s32[4,384]{1,0:T(4,128)} %bitcast.19, bf16[384,384]{1,0:T(8,128)(2,1)} %bitcast.16, bf16[384,384]{1,0:T(8,128)(2,1)} %bitcast.15), custom_call_target="tpu_custom_call" | custom-call | flops 226492416 | bytes 2359296 | tf_op jit(solution)/shard_map/pallas_call | solution.py:124
  13.0 1.6 %collective-permute-start.4 = (bf16[64,384]{1,0:T(8,128)(2,1)S(1)}, bf16[64,384]{1,0:T(8,128)(2,1)S(1)}, u32[]{:S(2)}, u32[]{:S(2)}) collective-permute-start(bf16[64,384]{1,0:T(8,128)(2,1)S(1)} %shard_map.67.rows_ref), channel_id=1, source_target_pairs={{0,1},{1,3},{2,0},{3,2},{4,5},{5,7},{6,4},{7,6},{8,9},{9,11},{10,8... | collective-permute-start | bytes 147464 | tf_op jit(solution)/shard_map/ppermute | solution.py:227
  14.6 1.5 %collective-permute-start.12 = (bf16[64,384]{1,0:T(8,128)(2,1)S(1)}, bf16[64,384]{1,0:T(8,128)(2,1)S(1)}, u32[]{:S(2)}, u32[]{:S(2)}) collective-permute-start(bf16[64,384]{1,0:T(8,128)(2,1)S(1)} %shard_map.76.rows_ref), channel_id=1, source_target_pairs={{0,1},{1,3},{2,0},{3,2},{4,5},{5,7},{6,4},{7,6},{8,9},{9,11},{10,8... | collective-permute-start | bytes 147464 | tf_op jit(solution)/shard_map/ppermute | solution.py:227
  16.1 1.0 %collective-permute-done.4.partner_ref = bf16[64,384]{1,0:T(8,128)(2,1)S(1)} collective-permute-done((bf16[64,384]{1,0:T(8,128)(2,1)S(1)}, bf16[64,384]{1,0:T(8,128)(2,1)S(1)}, u32[]{:S(2)}, u32[]{:S(2)}) %collective-permute-start.4) | collective-permute-done | bytes 49184 | tf_op jit(solution)/shard_map/ppermute | solution.py:227
  17.1 1.6 %collective-permute-start.6 = (bf16[64,384]{1,0:T(8,128)(2,1)S(1)}, bf16[64,384]{1,0:T(8,128)(2,1)S(1)}, u32[]{:S(2)}, u32[]{:S(2)}) collective-permute-start(bf16[64,384]{1,0:T(8,128)(2,1)S(1)} %shard_map.69.rows_ref), channel_id=1, source_target_pairs={{0,1},{1,3},{2,0},{3,2},{4,5},{5,7},{6,4},{7,6},{8,9},{9,11},{10,8... | collective-permute-start | bytes 147464 | tf_op jit(solution)/shard_map/ppermute | solution.py:227
  18.7 1.5 %collective-permute-start.13 = (bf16[64,384]{1,0:T(8,128)(2,1)S(1)}, bf16[64,384]{1,0:T(8,128)(2,1)S(1)}, u32[]{:S(2)}, u32[]{:S(2)}) collective-permute-start(bf16[64,384]{1,0:T(8,128)(2,1)S(1)} %shard_map.77.rows_ref), channel_id=1, source_target_pairs={{0,1},{1,3},{2,0},{3,2},{4,5},{5,7},{6,4},{7,6},{8,9},{9,11},{10,8... | collective-permute-start | bytes 147464 | tf_op jit(solution)/shard_map/ppermute | solution.py:227
  20.2 1.0 %collective-permute-done.6.partner_ref = bf16[64,384]{1,0:T(8,128)(2,1)S(1)} collective-permute-done((bf16[64,384]{1,0:T(8,128)(2,1)S(1)}, bf16[64,384]{1,0:T(8,128)(2,1)S(1)}, u32[]{:S(2)}, u32[]{:S(2)}) %collective-permute-start.6) | collective-permute-done | bytes 49184 | tf_op jit(solution)/shard_map/ppermute | solution.py:227
  21.2 1.6 %collective-permute-start.8 = (bf16[64,384]{1,0:T(8,128)(2,1)S(1)}, bf16[64,384]{1,0:T(8,128)(2,1)S(1)}, u32[]{:S(2)}, u32[]{:S(2)}) collective-permute-start(bf16[64,384]{1,0:T(8,128)(2,1)S(1)} %shard_map.71.rows_ref), channel_id=1, source_target_pairs={{0,1},{1,3},{2,0},{3,2},{4,5},{5,7},{6,4},{7,6},{8,9},{9,11},{10,8... | collective-permute-start | bytes 147464 | tf_op jit(solution)/shard_map/ppermute | solution.py:227
  22.8 1.5 %collective-permute-start.14 = (bf16[64,384]{1,0:T(8,128)(2,1)S(1)}, bf16[64,384]{1,0:T(8,128)(2,1)S(1)}, u32[]{:S(2)}, u32[]{:S(2)}) collective-permute-start(bf16[64,384]{1,0:T(8,128)(2,1)S(1)} %shard_map.79.rows_ref), channel_id=1, source_target_pairs={{0,1},{1,3},{2,0},{3,2},{4,5},{5,7},{6,4},{7,6},{8,9},{9,11},{10,8... | collective-permute-start | bytes 147464 | tf_op jit(solution)/shard_map/ppermute | solution.py:227
  24.3 1.0 %collective-permute-done.8.partner_ref = bf16[64,384]{1,0:T(8,128)(2,1)S(1)} collective-permute-done((bf16[64,384]{1,0:T(8,128)(2,1)S(1)}, bf16[64,384]{1,0:T(8,128)(2,1)S(1)}, u32[]{:S(2)}, u32[]{:S(2)}) %collective-permute-start.8) | collective-permute-done | bytes 49184 | tf_op jit(solution)/shard_map/ppermute | solution.py:227
  25.3 1.6 %collective-permute-start.9 = (bf16[64,384]{1,0:T(8,128)(2,1)S(1)}, bf16[64,384]{1,0:T(8,128)(2,1)S(1)}, u32[]{:S(2)}, u32[]{:S(2)}) collective-permute-start(bf16[64,384]{1,0:T(8,128)(2,1)S(1)} %shard_map.72.rows_ref), channel_id=1, source_target_pairs={{0,1},{1,3},{2,0},{3,2},{4,5},{5,7},{6,4},{7,6},{8,9},{9,11},{10,8... | collective-permute-start | bytes 147464 | tf_op jit(solution)/shard_map/ppermute | solution.py:227
  26.9 1.9 %collective-permute-start.15 = (bf16[64,384]{1,0:T(8,128)(2,1)S(1)}, bf16[64,384]{1,0:T(8,128)(2,1)S(1)}, u32[]{:S(2)}, u32[]{:S(2)}) collective-permute-start(bf16[64,384]{1,0:T(8,128)(2,1)S(1)} %shard_map.80.rows_ref), channel_id=1, source_target_pairs={{0,1},{1,3},{2,0},{3,2},{4,5},{5,7},{6,4},{7,6},{8,9},{9,11},{10,8... | collective-permute-start | bytes 147464 | tf_op jit(solution)/shard_map/ppermute | solution.py:227
  29.4 1.6 %collective-permute-start.10 = (bf16[64,384]{1,0:T(8,128)(2,1)S(1)}, bf16[64,384]{1,0:T(8,128)(2,1)S(1)}, u32[]{:S(2)}, u32[]{:S(2)}) collective-permute-start(bf16[64,384]{1,0:T(8,128)(2,1)S(1)} %shard_map.73.rows_ref), channel_id=1, source_target_pairs={{0,1},{1,3},{2,0},{3,2},{4,5},{5,7},{6,4},{7,6},{8,9},{9,11},{10,8... | collective-permute-start | bytes 147464 | tf_op jit(solution)/shard_map/ppermute | solution.py:227
  31.0 1.9 %collective-permute-start.18 = (bf16[64,384]{1,0:T(8,128)(2,1)S(1)}, bf16[64,384]{1,0:T(8,128)(2,1)S(1)}, u32[]{:S(2)}, u32[]{:S(2)}) collective-permute-start(bf16[64,384]{1,0:T(8,128)(2,1)S(1)} %shard_map.81.rows_ref), channel_id=1, source_target_pairs={{0,1},{1,3},{2,0},{3,2},{4,5},{5,7},{6,4},{7,6},{8,9},{9,11},{10,8... | collective-permute-start | bytes 147464 | tf_op jit(solution)/shard_map/ppermute | solution.py:227
  32.9 0.7 %shard_map.82._ = bf16[128,384]{1,0:T(8,128)(2,1)} custom-call(bf16[64,384]{1,0:T(8,128)(2,1)S(1)} %collective-permute-done.16.first, bf16[64,384]{1,0:T(8,128)(2,1)S(1)} %collective-permute-done.17.second), custom_call_target="tpu_custom_call" | custom-call | bytes 196608 | tf_op jit(solution)/shard_map/pallas_call | solution.py:195
  33.6 1.4 %collective-permute-start.11 = (bf16[64,384]{1,0:T(8,128)(2,1)S(1)}, bf16[64,384]{1,0:T(8,128)(2,1)S(1)}, u32[]{:S(2)}, u32[]{:S(2)}) collective-permute-start(bf16[64,384]{1,0:T(8,128)(2,1)S(1)} %shard_map.74.rows_ref), channel_id=1, source_target_pairs={{0,1},{1,3},{2,0},{3,2},{4,5},{5,7},{6,4},{7,6},{8,9},{9,11},{10,8... | collective-permute-start | bytes 147464 | tf_op jit(solution)/shard_map/ppermute | solution.py:227
  35.1 1.9 %collective-permute-start.19 = (bf16[64,384]{1,0:T(8,128)(2,1)S(1)}, bf16[64,384]{1,0:T(8,128)(2,1)S(1)}, u32[]{:S(2)}, u32[]{:S(2)}) collective-permute-start(bf16[64,384]{1,0:T(8,128)(2,1)S(1)} %shard_map.83.rows_ref), channel_id=1, source_target_pairs={{0,1},{1,3},{2,0},{3,2},{4,5},{5,7},{6,4},{7,6},{8,9},{9,11},{10,8... | collective-permute-start | bytes 147464 | tf_op jit(solution)/shard_map/ppermute | solution.py:227
  37.0 0.8 %collective-permute-done.11.partner_ref = bf16[64,384]{1,0:T(8,128)(2,1)S(1)} collective-permute-done((bf16[64,384]{1,0:T(8,128)(2,1)S(1)}, bf16[64,384]{1,0:T(8,128)(2,1)S(1)}, u32[]{:S(2)}, u32[]{:S(2)}) %collective-permute-start.11) | collective-permute-done | bytes 49184 | tf_op jit(solution)/shard_map/ppermute | solution.py:227
  37.8 1.4 %collective-permute-done.19.partner_ref = bf16[64,384]{1,0:T(8,128)(2,1)S(1)} collective-permute-done((bf16[64,384]{1,0:T(8,128)(2,1)S(1)}, bf16[64,384]{1,0:T(8,128)(2,1)S(1)}, u32[]{:S(2)}, u32[]{:S(2)}) %collective-permute-start.19) | collective-permute-done | bytes 49184 | tf_op jit(solution)/shard_map/ppermute | solution.py:227
  (38 shorter events, 2.2 us)
Async XLA Ops:
  1.3 5.6 %collective-permute-start = (bf16[128,384]{1,0:T(8,128)(2,1)S(1)}, bf16[128,384]{1,0:T(8,128)(2,1)S(1)}, u32[]{:S(2)}, u32[]{:S(2)}) collective-permute-start(bf16[128,384]{1,0:T(8,128)(2,1)S(1)} %shard_map.64.rows_ref.x_ref), channel_id=1, source_target_pairs={{0,1},{1,0},{2,3},{3,2},{4,5},{5,4},{6,7},{7,6},{8,9},{9,8},{10,11... | collective-permute-start | bytes 294920 | tf_op jit(solution)/shard_map/ppermute | solution.py:227
  7.1 5.3 %collective-permute-start.3 = (bf16[2,384,384]{2,1,0:T(8,128)(2,1)S(1)}, bf16[2,384,384]{2,1,0:T(8,128)(2,1)S(1)}, u32[]{:S(2)}, u32[]{:S(2)}) collective-permute-start(bf16[2,384,384]{2,1,0:T(8,128)(2,1)S(1)} %get-tuple-element.37.table_ref), channel_id=1, source_target_pairs={{0,16},{1,17},{2,18},{3,19},{4,20},{5,21},{6,22},{7,23},{8,24},{9,... | collective-permute-start | bytes 1769480 | tf_op jit(solution)/shard_map/ppermute | solution.py:227
  7.2 5.2 %collective-permute-start.2 = (bf16[128,384]{1,0:T(8,128)(2,1)S(1)}, bf16[128,384]{1,0:T(8,128)(2,1)S(1)}, u32[]{:S(2)}, u32[]{:S(2)}) collective-permute-start(bf16[128,384]{1,0:T(8,128)(2,1)S(1)} %shard_map.66), channel_id=1, source_target_pairs={{0,18},{1,19},{2,16},{3,17},{4,22},{5,23},{6,20},{7,21},{8,26},{9,... | collective-permute-start | bytes 294920 | tf_op jit(solution)/shard_map/ppermute | solution.py:227
  9.4 3.1 %collective-permute-start.1 = (bf16[128,384]{1,0:T(8,128)(2,1)S(1)}, bf16[128,384]{1,0:T(8,128)(2,1)S(1)}, u32[]{:S(2)}, u32[]{:S(2)}) collective-permute-start(bf16[128,384]{1,0:T(8,128)(2,1)S(1)} %shard_map.66), channel_id=1, source_target_pairs={{0,16},{1,17},{2,18},{3,19},{4,20},{5,21},{6,22},{7,23},{8,24},{9,... | collective-permute-start | bytes 294920 | tf_op jit(solution)/shard_map/ppermute | solution.py:227
  12.4 4.7 %collective-permute-start.5 = (bf16[2,384,384]{2,1,0:T(8,128)(2,1)S(1)}, bf16[2,384,384]{2,1,0:T(8,128)(2,1)S(1)}, u32[]{:S(2)}, u32[]{:S(2)}) collective-permute-start(bf16[2,384,384]{2,1,0:T(8,128)(2,1)S(1)} %get-tuple-element.45.table_ref), channel_id=1, source_target_pairs={{0,16},{1,17},{2,18},{3,19},{4,20},{5,21},{6,22},{7,23},{8,24},{9,... | collective-permute-start | bytes 1769480 | tf_op jit(solution)/shard_map/ppermute | solution.py:227
  12.8 7.4 %collective-permute-start.7 = (bf16[2,384,384]{2,1,0:T(8,128)(2,1)S(1)}, bf16[2,384,384]{2,1,0:T(8,128)(2,1)S(1)}, u32[]{:S(2)}, u32[]{:S(2)}) collective-permute-start(bf16[2,384,384]{2,1,0:T(8,128)(2,1)S(1)} %get-tuple-element.46.table_ref), channel_id=1, source_target_pairs={{0,16},{1,17},{2,18},{3,19},{4,20},{5,21},{6,22},{7,23},{8,24},{9,... | collective-permute-start | bytes 1769480 | tf_op jit(solution)/shard_map/ppermute | solution.py:227
  13.0 4.1 %collective-permute-start.4 = (bf16[64,384]{1,0:T(8,128)(2,1)S(1)}, bf16[64,384]{1,0:T(8,128)(2,1)S(1)}, u32[]{:S(2)}, u32[]{:S(2)}) collective-permute-start(bf16[64,384]{1,0:T(8,128)(2,1)S(1)} %shard_map.67.rows_ref), channel_id=1, source_target_pairs={{0,1},{1,3},{2,0},{3,2},{4,5},{5,7},{6,4},{7,6},{8,9},{9,11},{10,8... | collective-permute-start | bytes 147464 | tf_op jit(solution)/shard_map/ppermute | solution.py:227
  14.6 4.1 %collective-permute-start.12 = (bf16[64,384]{1,0:T(8,128)(2,1)S(1)}, bf16[64,384]{1,0:T(8,128)(2,1)S(1)}, u32[]{:S(2)}, u32[]{:S(2)}) collective-permute-start(bf16[64,384]{1,0:T(8,128)(2,1)S(1)} %shard_map.76.rows_ref), channel_id=1, source_target_pairs={{0,1},{1,3},{2,0},{3,2},{4,5},{5,7},{6,4},{7,6},{8,9},{9,11},{10,8... | collective-permute-start | bytes 147464 | tf_op jit(solution)/shard_map/ppermute | solution.py:227
  17.1 4.1 %collective-permute-start.6 = (bf16[64,384]{1,0:T(8,128)(2,1)S(1)}, bf16[64,384]{1,0:T(8,128)(2,1)S(1)}, u32[]{:S(2)}, u32[]{:S(2)}) collective-permute-start(bf16[64,384]{1,0:T(8,128)(2,1)S(1)} %shard_map.69.rows_ref), channel_id=1, source_target_pairs={{0,1},{1,3},{2,0},{3,2},{4,5},{5,7},{6,4},{7,6},{8,9},{9,11},{10,8... | collective-permute-start | bytes 147464 | tf_op jit(solution)/shard_map/ppermute | solution.py:227
  18.7 4.1 %collective-permute-start.13 = (bf16[64,384]{1,0:T(8,128)(2,1)S(1)}, bf16[64,384]{1,0:T(8,128)(2,1)S(1)}, u32[]{:S(2)}, u32[]{:S(2)}) collective-permute-start(bf16[64,384]{1,0:T(8,128)(2,1)S(1)} %shard_map.77.rows_ref), channel_id=1, source_target_pairs={{0,1},{1,3},{2,0},{3,2},{4,5},{5,7},{6,4},{7,6},{8,9},{9,11},{10,8... | collective-permute-start | bytes 147464 | tf_op jit(solution)/shard_map/ppermute | solution.py:227
  21.2 4.1 %collective-permute-start.8 = (bf16[64,384]{1,0:T(8,128)(2,1)S(1)}, bf16[64,384]{1,0:T(8,128)(2,1)S(1)}, u32[]{:S(2)}, u32[]{:S(2)}) collective-permute-start(bf16[64,384]{1,0:T(8,128)(2,1)S(1)} %shard_map.71.rows_ref), channel_id=1, source_target_pairs={{0,1},{1,3},{2,0},{3,2},{4,5},{5,7},{6,4},{7,6},{8,9},{9,11},{10,8... | collective-permute-start | bytes 147464 | tf_op jit(solution)/shard_map/ppermute | solution.py:227
  22.8 4.1 %collective-permute-start.14 = (bf16[64,384]{1,0:T(8,128)(2,1)S(1)}, bf16[64,384]{1,0:T(8,128)(2,1)S(1)}, u32[]{:S(2)}, u32[]{:S(2)}) collective-permute-start(bf16[64,384]{1,0:T(8,128)(2,1)S(1)} %shard_map.79.rows_ref), channel_id=1, source_target_pairs={{0,1},{1,3},{2,0},{3,2},{4,5},{5,7},{6,4},{7,6},{8,9},{9,11},{10,8... | collective-permute-start | bytes 147464 | tf_op jit(solution)/shard_map/ppermute | solution.py:227
  25.3 4.1 %collective-permute-start.9 = (bf16[64,384]{1,0:T(8,128)(2,1)S(1)}, bf16[64,384]{1,0:T(8,128)(2,1)S(1)}, u32[]{:S(2)}, u32[]{:S(2)}) collective-permute-start(bf16[64,384]{1,0:T(8,128)(2,1)S(1)} %shard_map.72.rows_ref), channel_id=1, source_target_pairs={{0,1},{1,3},{2,0},{3,2},{4,5},{5,7},{6,4},{7,6},{8,9},{9,11},{10,8... | collective-permute-start | bytes 147464 | tf_op jit(solution)/shard_map/ppermute | solution.py:227
  26.9 4.1 %collective-permute-start.15 = (bf16[64,384]{1,0:T(8,128)(2,1)S(1)}, bf16[64,384]{1,0:T(8,128)(2,1)S(1)}, u32[]{:S(2)}, u32[]{:S(2)}) collective-permute-start(bf16[64,384]{1,0:T(8,128)(2,1)S(1)} %shard_map.80.rows_ref), channel_id=1, source_target_pairs={{0,1},{1,3},{2,0},{3,2},{4,5},{5,7},{6,4},{7,6},{8,9},{9,11},{10,8... | collective-permute-start | bytes 147464 | tf_op jit(solution)/shard_map/ppermute | solution.py:227
  28.8 4.1 %collective-permute-start.16 = (bf16[64,384]{1,0:T(8,128)(2,1)S(1)}, bf16[64,384]{1,0:T(8,128)(2,1)S(1)}, u32[]{:S(2)}, u32[]{:S(2)}) collective-permute-start(bf16[64,384]{1,0:T(8,128)(2,1)S(1)} %shard_map.70.front_ref), channel_id=1, source_target_pairs={{0,16},{1,17},{2,18},{3,19},{4,20},{5,21},{6,22},{7,23},{8,24},{9,... | collective-permute-start | bytes 147464 | tf_op jit(solution)/shard_map/ppermute | solution.py:227
  28.8 4.1 %collective-permute-start.17 = (bf16[64,384]{1,0:T(8,128)(2,1)S(1)}, bf16[64,384]{1,0:T(8,128)(2,1)S(1)}, u32[]{:S(2)}, u32[]{:S(2)}) collective-permute-start(bf16[64,384]{1,0:T(8,128)(2,1)S(1)} %shard_map.78.front_ref), channel_id=1, source_target_pairs={{0,16},{1,17},{2,18},{3,19},{4,20},{5,21},{6,22},{7,23},{8,24},{9,... | collective-permute-start | bytes 147464 | tf_op jit(solution)/shard_map/ppermute | solution.py:227
  29.4 4.2 %collective-permute-start.10 = (bf16[64,384]{1,0:T(8,128)(2,1)S(1)}, bf16[64,384]{1,0:T(8,128)(2,1)S(1)}, u32[]{:S(2)}, u32[]{:S(2)}) collective-permute-start(bf16[64,384]{1,0:T(8,128)(2,1)S(1)} %shard_map.73.rows_ref), channel_id=1, source_target_pairs={{0,1},{1,3},{2,0},{3,2},{4,5},{5,7},{6,4},{7,6},{8,9},{9,11},{10,8... | collective-permute-start | bytes 147464 | tf_op jit(solution)/shard_map/ppermute | solution.py:227
  31.0 4.1 %collective-permute-start.18 = (bf16[64,384]{1,0:T(8,128)(2,1)S(1)}, bf16[64,384]{1,0:T(8,128)(2,1)S(1)}, u32[]{:S(2)}, u32[]{:S(2)}) collective-permute-start(bf16[64,384]{1,0:T(8,128)(2,1)S(1)} %shard_map.81.rows_ref), channel_id=1, source_target_pairs={{0,1},{1,3},{2,0},{3,2},{4,5},{5,7},{6,4},{7,6},{8,9},{9,11},{10,8... | collective-permute-start | bytes 147464 | tf_op jit(solution)/shard_map/ppermute | solution.py:227
  33.6 4.1 %collective-permute-start.11 = (bf16[64,384]{1,0:T(8,128)(2,1)S(1)}, bf16[64,384]{1,0:T(8,128)(2,1)S(1)}, u32[]{:S(2)}, u32[]{:S(2)}) collective-permute-start(bf16[64,384]{1,0:T(8,128)(2,1)S(1)} %shard_map.74.rows_ref), channel_id=1, source_target_pairs={{0,1},{1,3},{2,0},{3,2},{4,5},{5,7},{6,4},{7,6},{8,9},{9,11},{10,8... | collective-permute-start | bytes 147464 | tf_op jit(solution)/shard_map/ppermute | solution.py:227
  35.1 4.1 %collective-permute-start.19 = (bf16[64,384]{1,0:T(8,128)(2,1)S(1)}, bf16[64,384]{1,0:T(8,128)(2,1)S(1)}, u32[]{:S(2)}, u32[]{:S(2)}) collective-permute-start(bf16[64,384]{1,0:T(8,128)(2,1)S(1)} %shard_map.83.rows_ref), channel_id=1, source_target_pairs={{0,1},{1,3},{2,0},{3,2},{4,5},{5,7},{6,4},{7,6},{8,9},{9,11},{10,8... | collective-permute-start | bytes 147464 | tf_op jit(solution)/shard_map/ppermute | solution.py:227

commit v2 on v1

--- a/solution.py
+++ b/solution.py
@@ -230,7 +230,8 @@
 def swap(value, bit, row):
     def target(s, l):
         ring = 2 if (l ^ l >> 1) & 1 else 1
-        return s, l ^ (bit if s == row else ring)
+        idle = 3 - bit if bit < 3 else ring
+        return s, l ^ (bit if s == row else idle)
 
     return permute(value, target)
 

time: 39.5 us -> 39.5 us (level)
  waiting for transfers between devices: 6.51 us -> 8.76 us
  starting transfers between devices: 26.2 us -> 24 us
    ppermute x20, waiting for transfers between devices: 6.51 us -> 8.76 us  [permute(): return lax.ppermute(value, ('sweep', 'leaf'), pairs)]
    ppermute x20, starting transfers between devices: 26.2 us -> 24 us  [permute(): return lax.ppermute(value, ('sweep', 'leaf'), pairs)]
  transfers between devices with their start and end apart: 20 -> 20, of which waited for: 7 -> 9; matrix products, arithmetic and copies ran while one was open for 0% -> 0% of each run, Pallas kernels for 12% -> 12%
where the time goes in v2:
time: 39.5 us; the launch traced here: 39.2 us
  starting transfers between devices  24 us (61%)
  waiting for transfers between devices  8.76 us (22%)
  Pallas kernels  6.38 us (16%)
    ppermute x20, starting transfers between devices, permute(): return lax.ppermute(value, ('sweep', 'leaf'), pairs)  24 us
    ppermute x20, waiting for transfers between devices, permute(): return lax.ppermute(value, ('sweep', 'leaf'), pairs)  8.76 us
    pallas_call x2, Pallas kernels, prepare(): pl.pallas_call(lambda *refs: prepare_kernel(levels, single, more, *refs),...  4.18 us
    pallas_call x1, Pallas kernels, load(): pl.pallas_call(load_kernel, out_shape=pltpu.VMEM(rows.shape, BF), in_spec...  1.24 us
  transfers between devices with their start and end apart: 20, of which 9 were waited for; matrix products, arithmetic and copies ran while one was open for 0% of the time, Pallas kernels for 12%

profile of v2, /device:TPU:0, one launch (start us, length us, event | category | flops | bytes accessed | tf_op | source)
XLA Modules:
  0.0 39.2 jit_solution(11013310288833696434)
XLA Ops:
  0.0 1.2 %shard_map.64.rows_ref.x_ref = bf16[128,384]{1,0:T(8,128)(2,1)S(1)} custom-call(bf16[128,384]{1,0:T(8,128)(2,1)} %bitcast.17, bf16[384,384]{1,0:T(8,128)(2,1)} %bitcast.14), custom_call_target="tpu_custom_call" | custom-call | flops 37748736 | bytes 491520 | tf_op jit(solution)/shard_map/pallas_call | solution.py:59
  1.3 3.0 %collective-permute-start = (bf16[128,384]{1,0:T(8,128)(2,1)S(1)}, bf16[128,384]{1,0:T(8,128)(2,1)S(1)}, u32[]{:S(2)}, u32[]{:S(2)}) collective-permute-start(bf16[128,384]{1,0:T(8,128)(2,1)S(1)} %shard_map.64.rows_ref.x_ref), channel_id=1, source_target_pairs={{0,1},{1,0},{2,3},{3,2},{4,5},{5,4},{6,7},{7,6},{8,9},{9,8},{10,11... | collective-permute-start | bytes 294920 | tf_op jit(solution)/shard_map/ppermute | solution.py:227
  4.3 1.8 %shard_map.65 = (bf16[2,384,384]{2,1,0:T(8,128)(2,1)S(1)}, bf16[2,384,384]{2,1,0:T(8,128)(2,1)S(1)}) custom-call(bf16[4,384,384]{2,1,0:T(8,128)(2,1)} %bitcast.10, bf16[4,384,384]{2,1,0:T(8,128)(2,1)} %bitcast.12, s32[4,384]{1,0:T(4,128)} %bitcast.18), custom_call_target="tpu_custom_call" | custom-call | flops 226492416 | bytes 2359296 | tf_op jit(solution)/shard_map/pallas_call | solution.py:124
  6.1 0.8 %collective-permute-done.partner_ref = bf16[128,384]{1,0:T(8,128)(2,1)S(1)} collective-permute-done((bf16[128,384]{1,0:T(8,128)(2,1)S(1)}, bf16[128,384]{1,0:T(8,128)(2,1)S(1)}, u32[]{:S(2)}, u32[]{:S(2)}) %collective-permute-start) | collective-permute-done | bytes 98336 | tf_op jit(solution)/shard_map/ppermute | solution.py:227
  7.2 2.2 %collective-permute-start.2 = (bf16[128,384]{1,0:T(8,128)(2,1)S(1)}, bf16[128,384]{1,0:T(8,128)(2,1)S(1)}, u32[]{:S(2)}, u32[]{:S(2)}) collective-permute-start(bf16[128,384]{1,0:T(8,128)(2,1)S(1)} %shard_map.66), channel_id=1, source_target_pairs={{0,18},{1,19},{2,16},{3,17},{4,22},{5,23},{6,20},{7,21},{8,26},{9,... | collective-permute-start | bytes 294920 | tf_op jit(solution)/shard_map/ppermute | solution.py:227
  9.4 2.4 %shard_map.68 = (bf16[2,384,384]{2,1,0:T(8,128)(2,1)S(1)}, bf16[2,384,384]{2,1,0:T(8,128)(2,1)S(1)}, bf16[384,384]{1,0:T(8,128)(2,1)S(1)}) custom-call(bf16[4,384,384]{2,1,0:T(8,128)(2,1)} %bitcast.11, bf16[4,384,384]{2,1,0:T(8,128)(2,1)} %bitcast.13, s32[4,384]{1,0:T(4,128)} %bitcast.19, bf16[384,384]{1,0:T(8,128)(2,1)} %bitcast.16, bf16[384,384]{1,0:T(8,128)(2,1)} %bitcast.15), custom_call_target="tpu_custom_call" | custom-call | flops 226492416 | bytes 2359296 | tf_op jit(solution)/shard_map/pallas_call | solution.py:124
  11.8 0.6 %collective-permute-done.2.partner_ref = bf16[128,384]{1,0:T(8,128)(2,1)S(1)} collective-permute-done((bf16[128,384]{1,0:T(8,128)(2,1)S(1)}, bf16[128,384]{1,0:T(8,128)(2,1)S(1)}, u32[]{:S(2)}, u32[]{:S(2)}) %collective-permute-start.2) | collective-permute-done | bytes 98336 | tf_op jit(solution)/shard_map/ppermute | solution.py:227
  13.0 1.6 %collective-permute-start.4 = (bf16[64,384]{1,0:T(8,128)(2,1)S(1)}, bf16[64,384]{1,0:T(8,128)(2,1)S(1)}, u32[]{:S(2)}, u32[]{:S(2)}) collective-permute-start(bf16[64,384]{1,0:T(8,128)(2,1)S(1)} %shard_map.67.rows_ref), channel_id=1, source_target_pairs={{0,1},{1,3},{2,0},{3,2},{4,5},{5,7},{6,4},{7,6},{8,9},{9,11},{10,8... | collective-permute-start | bytes 147464 | tf_op jit(solution)/shard_map/ppermute | solution.py:227
  14.6 1.5 %collective-permute-start.12 = (bf16[64,384]{1,0:T(8,128)(2,1)S(1)}, bf16[64,384]{1,0:T(8,128)(2,1)S(1)}, u32[]{:S(2)}, u32[]{:S(2)}) collective-permute-start(bf16[64,384]{1,0:T(8,128)(2,1)S(1)} %shard_map.76.rows_ref), channel_id=1, source_target_pairs={{0,1},{1,3},{2,0},{3,2},{4,5},{5,7},{6,4},{7,6},{8,9},{9,11},{10,8... | collective-permute-start | bytes 147464 | tf_op jit(solution)/shard_map/ppermute | solution.py:227
  16.1 1.0 %collective-permute-done.4.partner_ref = bf16[64,384]{1,0:T(8,128)(2,1)S(1)} collective-permute-done((bf16[64,384]{1,0:T(8,128)(2,1)S(1)}, bf16[64,384]{1,0:T(8,128)(2,1)S(1)}, u32[]{:S(2)}, u32[]{:S(2)}) %collective-permute-start.4) | collective-permute-done | bytes 49184 | tf_op jit(solution)/shard_map/ppermute | solution.py:227
  17.1 1.6 %collective-permute-start.6 = (bf16[64,384]{1,0:T(8,128)(2,1)S(1)}, bf16[64,384]{1,0:T(8,128)(2,1)S(1)}, u32[]{:S(2)}, u32[]{:S(2)}) collective-permute-start(bf16[64,384]{1,0:T(8,128)(2,1)S(1)} %shard_map.69.rows_ref), channel_id=1, source_target_pairs={{0,1},{1,3},{2,0},{3,2},{4,5},{5,7},{6,4},{7,6},{8,9},{9,11},{10,8... | collective-permute-start | bytes 147464 | tf_op jit(solution)/shard_map/ppermute | solution.py:227
  18.7 1.5 %collective-permute-start.13 = (bf16[64,384]{1,0:T(8,128)(2,1)S(1)}, bf16[64,384]{1,0:T(8,128)(2,1)S(1)}, u32[]{:S(2)}, u32[]{:S(2)}) collective-permute-start(bf16[64,384]{1,0:T(8,128)(2,1)S(1)} %shard_map.77.rows_ref), channel_id=1, source_target_pairs={{0,1},{1,3},{2,0},{3,2},{4,5},{5,7},{6,4},{7,6},{8,9},{9,11},{10,8... | collective-permute-start | bytes 147464 | tf_op jit(solution)/shard_map/ppermute | solution.py:227
  20.2 1.0 %collective-permute-done.6.partner_ref = bf16[64,384]{1,0:T(8,128)(2,1)S(1)} collective-permute-done((bf16[64,384]{1,0:T(8,128)(2,1)S(1)}, bf16[64,384]{1,0:T(8,128)(2,1)S(1)}, u32[]{:S(2)}, u32[]{:S(2)}) %collective-permute-start.6) | collective-permute-done | bytes 49184 | tf_op jit(solution)/shard_map/ppermute | solution.py:227
  21.2 1.6 %collective-permute-start.8 = (bf16[64,384]{1,0:T(8,128)(2,1)S(1)}, bf16[64,384]{1,0:T(8,128)(2,1)S(1)}, u32[]{:S(2)}, u32[]{:S(2)}) collective-permute-start(bf16[64,384]{1,0:T(8,128)(2,1)S(1)} %shard_map.71.rows_ref), channel_id=1, source_target_pairs={{0,2},{1,3},{2,0},{3,1},{4,6},{5,7},{6,4},{7,5},{8,10},{9,11},{10,... | collective-permute-start | bytes 147464 | tf_op jit(solution)/shard_map/ppermute | solution.py:227
  23.3 1.9 %collective-permute-done.8.partner_ref = bf16[64,384]{1,0:T(8,128)(2,1)S(1)} collective-permute-done((bf16[64,384]{1,0:T(8,128)(2,1)S(1)}, bf16[64,384]{1,0:T(8,128)(2,1)S(1)}, u32[]{:S(2)}, u32[]{:S(2)}) %collective-permute-start.8) | collective-permute-done | bytes 49184 | tf_op jit(solution)/shard_map/ppermute | solution.py:227
  25.3 1.6 %collective-permute-start.9 = (bf16[64,384]{1,0:T(8,128)(2,1)S(1)}, bf16[64,384]{1,0:T(8,128)(2,1)S(1)}, u32[]{:S(2)}, u32[]{:S(2)}) collective-permute-start(bf16[64,384]{1,0:T(8,128)(2,1)S(1)} %shard_map.72.rows_ref), channel_id=1, source_target_pairs={{0,1},{1,0},{2,3},{3,2},{4,5},{5,4},{6,7},{7,6},{8,9},{9,8},{10,11... | collective-permute-start | bytes 147464 | tf_op jit(solution)/shard_map/ppermute | solution.py:227
  26.9 1.5 %collective-permute-start.15 = (bf16[64,384]{1,0:T(8,128)(2,1)S(1)}, bf16[64,384]{1,0:T(8,128)(2,1)S(1)}, u32[]{:S(2)}, u32[]{:S(2)}) collective-permute-start(bf16[64,384]{1,0:T(8,128)(2,1)S(1)} %shard_map.80.rows_ref), channel_id=1, source_target_pairs={{0,1},{1,0},{2,3},{3,2},{4,5},{5,4},{6,7},{7,6},{8,9},{9,8},{10,11... | collective-permute-start | bytes 147464 | tf_op jit(solution)/shard_map/ppermute | solution.py:227
  29.4 1.6 %collective-permute-start.10 = (bf16[64,384]{1,0:T(8,128)(2,1)S(1)}, bf16[64,384]{1,0:T(8,128)(2,1)S(1)}, u32[]{:S(2)}, u32[]{:S(2)}) collective-permute-start(bf16[64,384]{1,0:T(8,128)(2,1)S(1)} %shard_map.73.rows_ref), channel_id=1, source_target_pairs={{0,1},{1,3},{2,0},{3,2},{4,5},{5,7},{6,4},{7,6},{8,9},{9,11},{10,8... | collective-permute-start | bytes 147464 | tf_op jit(solution)/shard_map/ppermute | solution.py:227
  31.0 1.5 %collective-permute-start.18 = (bf16[64,384]{1,0:T(8,128)(2,1)S(1)}, bf16[64,384]{1,0:T(8,128)(2,1)S(1)}, u32[]{:S(2)}, u32[]{:S(2)}) collective-permute-start(bf16[64,384]{1,0:T(8,128)(2,1)S(1)} %shard_map.81.rows_ref), channel_id=1, source_target_pairs={{0,1},{1,3},{2,0},{3,2},{4,5},{5,7},{6,4},{7,6},{8,9},{9,11},{10,8... | collective-permute-start | bytes 147464 | tf_op jit(solution)/shard_map/ppermute | solution.py:227
  32.5 0.7 %shard_map.82._ = bf16[128,384]{1,0:T(8,128)(2,1)} custom-call(bf16[64,384]{1,0:T(8,128)(2,1)S(1)} %collective-permute-done.16.first, bf16[64,384]{1,0:T(8,128)(2,1)S(1)} %collective-permute-done.17.second), custom_call_target="tpu_custom_call" | custom-call | bytes 196608 | tf_op jit(solution)/shard_map/pallas_call | solution.py:195
  33.5 1.6 %collective-permute-start.11 = (bf16[64,384]{1,0:T(8,128)(2,1)S(1)}, bf16[64,384]{1,0:T(8,128)(2,1)S(1)}, u32[]{:S(2)}, u32[]{:S(2)}) collective-permute-start(bf16[64,384]{1,0:T(8,128)(2,1)S(1)} %shard_map.74.rows_ref), channel_id=1, source_target_pairs={{0,1},{1,3},{2,0},{3,2},{4,5},{5,7},{6,4},{7,6},{8,9},{9,11},{10,8... | collective-permute-start | bytes 147464 | tf_op jit(solution)/shard_map/ppermute | solution.py:227
  35.1 1.5 %collective-permute-start.19 = (bf16[64,384]{1,0:T(8,128)(2,1)S(1)}, bf16[64,384]{1,0:T(8,128)(2,1)S(1)}, u32[]{:S(2)}, u32[]{:S(2)}) collective-permute-start(bf16[64,384]{1,0:T(8,128)(2,1)S(1)} %shard_map.83.rows_ref), channel_id=1, source_target_pairs={{0,1},{1,3},{2,0},{3,2},{4,5},{5,7},{6,4},{7,6},{8,9},{9,11},{10,8... | collective-permute-start | bytes 147464 | tf_op jit(solution)/shard_map/ppermute | solution.py:227
  36.6 1.0 %collective-permute-done.11.partner_ref = bf16[64,384]{1,0:T(8,128)(2,1)S(1)} collective-permute-done((bf16[64,384]{1,0:T(8,128)(2,1)S(1)}, bf16[64,384]{1,0:T(8,128)(2,1)S(1)}, u32[]{:S(2)}, u32[]{:S(2)}) %collective-permute-start.11) | collective-permute-done | bytes 49184 | tf_op jit(solution)/shard_map/ppermute | solution.py:227
  37.6 1.6 %collective-permute-done.19.partner_ref = bf16[64,384]{1,0:T(8,128)(2,1)S(1)} collective-permute-done((bf16[64,384]{1,0:T(8,128)(2,1)S(1)}, bf16[64,384]{1,0:T(8,128)(2,1)S(1)}, u32[]{:S(2)}, u32[]{:S(2)}) %collective-permute-start.19) | collective-permute-done | bytes 49184 | tf_op jit(solution)/shard_map/ppermute | solution.py:227
  (38 shorter events, 2.9 us)
Async XLA Ops:
  1.3 5.6 %collective-permute-start = (bf16[128,384]{1,0:T(8,128)(2,1)S(1)}, bf16[128,384]{1,0:T(8,128)(2,1)S(1)}, u32[]{:S(2)}, u32[]{:S(2)}) collective-permute-start(bf16[128,384]{1,0:T(8,128)(2,1)S(1)} %shard_map.64.rows_ref.x_ref), channel_id=1, source_target_pairs={{0,1},{1,0},{2,3},{3,2},{4,5},{5,4},{6,7},{7,6},{8,9},{9,8},{10,11... | collective-permute-start | bytes 294920 | tf_op jit(solution)/shard_map/ppermute | solution.py:227
  7.1 5.3 %collective-permute-start.3 = (bf16[2,384,384]{2,1,0:T(8,128)(2,1)S(1)}, bf16[2,384,384]{2,1,0:T(8,128)(2,1)S(1)}, u32[]{:S(2)}, u32[]{:S(2)}) collective-permute-start(bf16[2,384,384]{2,1,0:T(8,128)(2,1)S(1)} %get-tuple-element.37.table_ref), channel_id=1, source_target_pairs={{0,16},{1,17},{2,18},{3,19},{4,20},{5,21},{6,22},{7,23},{8,24},{9,... | collective-permute-start | bytes 1769480 | tf_op jit(solution)/shard_map/ppermute | solution.py:227
  7.2 5.2 %collective-permute-start.2 = (bf16[128,384]{1,0:T(8,128)(2,1)S(1)}, bf16[128,384]{1,0:T(8,128)(2,1)S(1)}, u32[]{:S(2)}, u32[]{:S(2)}) collective-permute-start(bf16[128,384]{1,0:T(8,128)(2,1)S(1)} %shard_map.66), channel_id=1, source_target_pairs={{0,18},{1,19},{2,16},{3,17},{4,22},{5,23},{6,20},{7,21},{8,26},{9,... | collective-permute-start | bytes 294920 | tf_op jit(solution)/shard_map/ppermute | solution.py:227
  9.4 3.1 %collective-permute-start.1 = (bf16[128,384]{1,0:T(8,128)(2,1)S(1)}, bf16[128,384]{1,0:T(8,128)(2,1)S(1)}, u32[]{:S(2)}, u32[]{:S(2)}) collective-permute-start(bf16[128,384]{1,0:T(8,128)(2,1)S(1)} %shard_map.66), channel_id=1, source_target_pairs={{0,16},{1,17},{2,18},{3,19},{4,20},{5,21},{6,22},{7,23},{8,24},{9,... | collective-permute-start | bytes 294920 | tf_op jit(solution)/shard_map/ppermute | solution.py:227
  12.4 4.7 %collective-permute-start.5 = (bf16[2,384,384]{2,1,0:T(8,128)(2,1)S(1)}, bf16[2,384,384]{2,1,0:T(8,128)(2,1)S(1)}, u32[]{:S(2)}, u32[]{:S(2)}) collective-permute-start(bf16[2,384,384]{2,1,0:T(8,128)(2,1)S(1)} %get-tuple-element.45.table_ref), channel_id=1, source_target_pairs={{0,16},{1,17},{2,18},{3,19},{4,20},{5,21},{6,22},{7,23},{8,24},{9,... | collective-permute-start | bytes 1769480 | tf_op jit(solution)/shard_map/ppermute | solution.py:227
  12.9 7.4 %collective-permute-start.7 = (bf16[2,384,384]{2,1,0:T(8,128)(2,1)S(1)}, bf16[2,384,384]{2,1,0:T(8,128)(2,1)S(1)}, u32[]{:S(2)}, u32[]{:S(2)}) collective-permute-start(bf16[2,384,384]{2,1,0:T(8,128)(2,1)S(1)} %get-tuple-element.46.table_ref), channel_id=1, source_target_pairs={{0,16},{1,17},{2,18},{3,19},{4,20},{5,21},{6,22},{7,23},{8,24},{9,... | collective-permute-start | bytes 1769480 | tf_op jit(solution)/shard_map/ppermute | solution.py:227
  13.0 4.1 %collective-permute-start.4 = (bf16[64,384]{1,0:T(8,128)(2,1)S(1)}, bf16[64,384]{1,0:T(8,128)(2,1)S(1)}, u32[]{:S(2)}, u32[]{:S(2)}) collective-permute-start(bf16[64,384]{1,0:T(8,128)(2,1)S(1)} %shard_map.67.rows_ref), channel_id=1, source_target_pairs={{0,1},{1,3},{2,0},{3,2},{4,5},{5,7},{6,4},{7,6},{8,9},{9,11},{10,8... | collective-permute-start | bytes 147464 | tf_op jit(solution)/shard_map/ppermute | solution.py:227
  14.6 4.1 %collective-permute-start.12 = (bf16[64,384]{1,0:T(8,128)(2,1)S(1)}, bf16[64,384]{1,0:T(8,128)(2,1)S(1)}, u32[]{:S(2)}, u32[]{:S(2)}) collective-permute-start(bf16[64,384]{1,0:T(8,128)(2,1)S(1)} %shard_map.76.rows_ref), channel_id=1, source_target_pairs={{0,1},{1,3},{2,0},{3,2},{4,5},{5,7},{6,4},{7,6},{8,9},{9,11},{10,8... | collective-permute-start | bytes 147464 | tf_op jit(solution)/shard_map/ppermute | solution.py:227
  17.1 4.1 %collective-permute-start.6 = (bf16[64,384]{1,0:T(8,128)(2,1)S(1)}, bf16[64,384]{1,0:T(8,128)(2,1)S(1)}, u32[]{:S(2)}, u32[]{:S(2)}) collective-permute-start(bf16[64,384]{1,0:T(8,128)(2,1)S(1)} %shard_map.69.rows_ref), channel_id=1, source_target_pairs={{0,1},{1,3},{2,0},{3,2},{4,5},{5,7},{6,4},{7,6},{8,9},{9,11},{10,8... | collective-permute-start | bytes 147464 | tf_op jit(solution)/shard_map/ppermute | solution.py:227
  18.7 4.1 %collective-permute-start.13 = (bf16[64,384]{1,0:T(8,128)(2,1)S(1)}, bf16[64,384]{1,0:T(8,128)(2,1)S(1)}, u32[]{:S(2)}, u32[]{:S(2)}) collective-permute-start(bf16[64,384]{1,0:T(8,128)(2,1)S(1)} %shard_map.77.rows_ref), channel_id=1, source_target_pairs={{0,1},{1,3},{2,0},{3,2},{4,5},{5,7},{6,4},{7,6},{8,9},{9,11},{10,8... | collective-permute-start | bytes 147464 | tf_op jit(solution)/shard_map/ppermute | solution.py:227
  21.2 4.1 %collective-permute-start.8 = (bf16[64,384]{1,0:T(8,128)(2,1)S(1)}, bf16[64,384]{1,0:T(8,128)(2,1)S(1)}, u32[]{:S(2)}, u32[]{:S(2)}) collective-permute-start(bf16[64,384]{1,0:T(8,128)(2,1)S(1)} %shard_map.71.rows_ref), channel_id=1, source_target_pairs={{0,2},{1,3},{2,0},{3,1},{4,6},{5,7},{6,4},{7,5},{8,10},{9,11},{10,... | collective-permute-start | bytes 147464 | tf_op jit(solution)/shard_map/ppermute | solution.py:227
  22.8 4.1 %collective-permute-start.14 = (bf16[64,384]{1,0:T(8,128)(2,1)S(1)}, bf16[64,384]{1,0:T(8,128)(2,1)S(1)}, u32[]{:S(2)}, u32[]{:S(2)}) collective-permute-start(bf16[64,384]{1,0:T(8,128)(2,1)S(1)} %shard_map.79.rows_ref), channel_id=1, source_target_pairs={{0,2},{1,3},{2,0},{3,1},{4,6},{5,7},{6,4},{7,5},{8,10},{9,11},{10,... | collective-permute-start | bytes 147464 | tf_op jit(solution)/shard_map/ppermute | solution.py:227
  25.3 4.1 %collective-permute-start.9 = (bf16[64,384]{1,0:T(8,128)(2,1)S(1)}, bf16[64,384]{1,0:T(8,128)(2,1)S(1)}, u32[]{:S(2)}, u32[]{:S(2)}) collective-permute-start(bf16[64,384]{1,0:T(8,128)(2,1)S(1)} %shard_map.72.rows_ref), channel_id=1, source_target_pairs={{0,1},{1,0},{2,3},{3,2},{4,5},{5,4},{6,7},{7,6},{8,9},{9,8},{10,11... | collective-permute-start | bytes 147464 | tf_op jit(solution)/shard_map/ppermute | solution.py:227
  26.9 4.1 %collective-permute-start.15 = (bf16[64,384]{1,0:T(8,128)(2,1)S(1)}, bf16[64,384]{1,0:T(8,128)(2,1)S(1)}, u32[]{:S(2)}, u32[]{:S(2)}) collective-permute-start(bf16[64,384]{1,0:T(8,128)(2,1)S(1)} %shard_map.80.rows_ref), channel_id=1, source_target_pairs={{0,1},{1,0},{2,3},{3,2},{4,5},{5,4},{6,7},{7,6},{8,9},{9,8},{10,11... | collective-permute-start | bytes 147464 | tf_op jit(solution)/shard_map/ppermute | solution.py:227
  28.4 4.1 %collective-permute-start.16 = (bf16[64,384]{1,0:T(8,128)(2,1)S(1)}, bf16[64,384]{1,0:T(8,128)(2,1)S(1)}, u32[]{:S(2)}, u32[]{:S(2)}) collective-permute-start(bf16[64,384]{1,0:T(8,128)(2,1)S(1)} %shard_map.70.front_ref), channel_id=1, source_target_pairs={{0,16},{1,17},{2,18},{3,19},{4,20},{5,21},{6,22},{7,23},{8,24},{9,... | collective-permute-start | bytes 147464 | tf_op jit(solution)/shard_map/ppermute | solution.py:227
  28.4 4.1 %collective-permute-start.17 = (bf16[64,384]{1,0:T(8,128)(2,1)S(1)}, bf16[64,384]{1,0:T(8,128)(2,1)S(1)}, u32[]{:S(2)}, u32[]{:S(2)}) collective-permute-start(bf16[64,384]{1,0:T(8,128)(2,1)S(1)} %shard_map.78.front_ref), channel_id=1, source_target_pairs={{0,16},{1,17},{2,18},{3,19},{4,20},{5,21},{6,22},{7,23},{8,24},{9,... | collective-permute-start | bytes 147464 | tf_op jit(solution)/shard_map/ppermute | solution.py:227
  29.4 4.1 %collective-permute-start.10 = (bf16[64,384]{1,0:T(8,128)(2,1)S(1)}, bf16[64,384]{1,0:T(8,128)(2,1)S(1)}, u32[]{:S(2)}, u32[]{:S(2)}) collective-permute-start(bf16[64,384]{1,0:T(8,128)(2,1)S(1)} %shard_map.73.rows_ref), channel_id=1, source_target_pairs={{0,1},{1,3},{2,0},{3,2},{4,5},{5,7},{6,4},{7,6},{8,9},{9,11},{10,8... | collective-permute-start | bytes 147464 | tf_op jit(solution)/shard_map/ppermute | solution.py:227
  31.0 4.1 %collective-permute-start.18 = (bf16[64,384]{1,0:T(8,128)(2,1)S(1)}, bf16[64,384]{1,0:T(8,128)(2,1)S(1)}, u32[]{:S(2)}, u32[]{:S(2)}) collective-permute-start(bf16[64,384]{1,0:T(8,128)(2,1)S(1)} %shard_map.81.rows_ref), channel_id=1, source_target_pairs={{0,1},{1,3},{2,0},{3,2},{4,5},{5,7},{6,4},{7,6},{8,9},{9,11},{10,8... | collective-permute-start | bytes 147464 | tf_op jit(solution)/shard_map/ppermute | solution.py:227
  33.5 4.1 %collective-permute-start.11 = (bf16[64,384]{1,0:T(8,128)(2,1)S(1)}, bf16[64,384]{1,0:T(8,128)(2,1)S(1)}, u32[]{:S(2)}, u32[]{:S(2)}) collective-permute-start(bf16[64,384]{1,0:T(8,128)(2,1)S(1)} %shard_map.74.rows_ref), channel_id=1, source_target_pairs={{0,1},{1,3},{2,0},{3,2},{4,5},{5,7},{6,4},{7,6},{8,9},{9,11},{10,8... | collective-permute-start | bytes 147464 | tf_op jit(solution)/shard_map/ppermute | solution.py:227
  35.1 4.1 %collective-permute-start.19 = (bf16[64,384]{1,0:T(8,128)(2,1)S(1)}, bf16[64,384]{1,0:T(8,128)(2,1)S(1)}, u32[]{:S(2)}, u32[]{:S(2)}) collective-permute-start(bf16[64,384]{1,0:T(8,128)(2,1)S(1)} %shard_map.83.rows_ref), channel_id=1, source_target_pairs={{0,1},{1,3},{2,0},{3,2},{4,5},{5,7},{6,4},{7,6},{8,9},{9,11},{10,8... | collective-permute-start | bytes 147464 | tf_op jit(solution)/shard_map/ppermute | solution.py:227

commit v3 on v1

--- a/solution.py
+++ b/solution.py
@@ -214,6 +214,33 @@
         compiler_params=pltpu.CompilerParams(vmem_limit_bytes=2 * MIB),
         cost_estimate=cost(0, 8 * blocks[0].size),
     )(*blocks, out)
+
+
+def finish(which, out, first, rows, partner, table, at):
+    half, width = rows.shape
+
+    def kernel(first_ref, rows_ref, partner_ref, table_ref, _, out_ref, second_ref, sems):
+        @pl.when(side() == which)
+        def _():
+            head = pltpu.make_async_copy(first_ref, out_ref.at[pl.ds(0, half)], sems.at[0])
+            head.start()
+            total = mm(rows_ref[...], table_ref[at]) + mm(partner_ref[...], table_ref[at + 1])
+            second_ref[...] = total.astype(BF)
+            tail = pltpu.make_async_copy(second_ref, out_ref.at[pl.ds(half, half)], sems.at[1])
+            tail.start()
+            head.wait()
+            tail.wait()
+
+    return pl.pallas_call(
+        kernel,
+        out_shape=pltpu.HBM(out.shape, BF),
+        in_specs=[VMEM] * 4 + [HBM],
+        out_specs=HBM,
+        scratch_shapes=[pltpu.VMEM((half, width), BF), pltpu.SemaphoreType.DMA((2,))],
+        input_output_aliases={4: 0},
+        compiler_params=pltpu.CompilerParams(vmem_limit_bytes=4 * MIB),
+        cost_estimate=cost(HINT, 8 * rows.size),
+    )(first, rows, partner, table, out)
 
 
 def permute(value, target):
@@ -297,6 +324,9 @@
                 if sections == 2:
                     out = write_first(0, back)
                     front[1], (out,) = behind(front[1], out)
+            if sections == 2 and section == 1 and j == count - 1:
+                head = level(1, front[0], partners[0], tables[j])
+                return finish(1, out, head, front[1], partners[1], tables[j], 0)[None, None]
             front = [level(1, part, came, tables[j]) for part, came in zip(front, partners)]
         if section % 2 == 0:
             back = front

time: 39.5 us -> 39.5 us (level)
  no operation moved by 1% of the time
where the time goes in v3:
time: 39.5 us; the launch traced here: 39.2 us
  starting transfers between devices  26.2 us (66%)
  waiting for transfers between devices  6.51 us (16%)
  Pallas kernels  6.4 us (16%)
    ppermute x20, starting transfers between devices, permute(): return lax.ppermute(value, ('sweep', 'leaf'), pairs)  26.2 us
    ppermute x20, waiting for transfers between devices, permute(): return lax.ppermute(value, ('sweep', 'leaf'), pairs)  6.51 us
    pallas_call x2, Pallas kernels, prepare(): pl.pallas_call(lambda *refs: prepare_kernel(levels, single, more, *refs),...  4.18 us
    pallas_call x1, Pallas kernels, load(): pl.pallas_call(load_kernel, out_shape=pltpu.VMEM(rows.shape, BF), in_spec...  1.24 us
  transfers between devices with their start and end apart: 20, of which 7 were waited for; matrix products, arithmetic and copies ran while one was open for 0% of the time, Pallas kernels for 12%

profile of v3, /device:TPU:0, one launch (start us, length us, event | category | flops | bytes accessed | tf_op | source)
XLA Modules:
  0.0 39.2 jit_solution(15045859031982133519)
XLA Ops:
  0.0 1.2 %shard_map.64.rows_ref.x_ref = bf16[128,384]{1,0:T(8,128)(2,1)S(1)} custom-call(bf16[128,384]{1,0:T(8,128)(2,1)} %bitcast.17, bf16[384,384]{1,0:T(8,128)(2,1)} %bitcast.14), custom_call_target="tpu_custom_call" | custom-call | flops 37748736 | bytes 491520 | tf_op jit(solution)/shard_map/pallas_call | solution.py:59
  1.3 3.0 %collective-permute-start = (bf16[128,384]{1,0:T(8,128)(2,1)S(1)}, bf16[128,384]{1,0:T(8,128)(2,1)S(1)}, u32[]{:S(2)}, u32[]{:S(2)}) collective-permute-start(bf16[128,384]{1,0:T(8,128)(2,1)S(1)} %shard_map.64.rows_ref.x_ref), channel_id=1, source_target_pairs={{0,1},{1,0},{2,3},{3,2},{4,5},{5,4},{6,7},{7,6},{8,9},{9,8},{10,11... | collective-permute-start | bytes 294920 | tf_op jit(solution)/shard_map/ppermute | solution.py:254
  4.2 1.8 %shard_map.65 = (bf16[2,384,384]{2,1,0:T(8,128)(2,1)S(1)}, bf16[2,384,384]{2,1,0:T(8,128)(2,1)S(1)}) custom-call(bf16[4,384,384]{2,1,0:T(8,128)(2,1)} %bitcast.10, bf16[4,384,384]{2,1,0:T(8,128)(2,1)} %bitcast.12, s32[4,384]{1,0:T(4,128)} %bitcast.18), custom_call_target="tpu_custom_call" | custom-call | flops 226492416 | bytes 2359296 | tf_op jit(solution)/shard_map/pallas_call | solution.py:124
  6.1 0.8 %collective-permute-done.partner_ref = bf16[128,384]{1,0:T(8,128)(2,1)S(1)} collective-permute-done((bf16[128,384]{1,0:T(8,128)(2,1)S(1)}, bf16[128,384]{1,0:T(8,128)(2,1)S(1)}, u32[]{:S(2)}, u32[]{:S(2)}) %collective-permute-start) | collective-permute-done | bytes 98336 | tf_op jit(solution)/shard_map/ppermute | solution.py:254
  7.2 2.2 %collective-permute-start.2 = (bf16[128,384]{1,0:T(8,128)(2,1)S(1)}, bf16[128,384]{1,0:T(8,128)(2,1)S(1)}, u32[]{:S(2)}, u32[]{:S(2)}) collective-permute-start(bf16[128,384]{1,0:T(8,128)(2,1)S(1)} %shard_map.66), channel_id=1, source_target_pairs={{0,18},{1,19},{2,16},{3,17},{4,22},{5,23},{6,20},{7,21},{8,26},{9,... | collective-permute-start | bytes 294920 | tf_op jit(solution)/shard_map/ppermute | solution.py:254
  9.4 2.4 %shard_map.68 = (bf16[2,384,384]{2,1,0:T(8,128)(2,1)S(1)}, bf16[2,384,384]{2,1,0:T(8,128)(2,1)S(1)}, bf16[384,384]{1,0:T(8,128)(2,1)S(1)}) custom-call(bf16[4,384,384]{2,1,0:T(8,128)(2,1)} %bitcast.11, bf16[4,384,384]{2,1,0:T(8,128)(2,1)} %bitcast.13, s32[4,384]{1,0:T(4,128)} %bitcast.19, bf16[384,384]{1,0:T(8,128)(2,1)} %bitcast.16, bf16[384,384]{1,0:T(8,128)(2,1)} %bitcast.15), custom_call_target="tpu_custom_call" | custom-call | flops 226492416 | bytes 2359296 | tf_op jit(solution)/shard_map/pallas_call | solution.py:124
  13.0 1.6 %collective-permute-start.4 = (bf16[64,384]{1,0:T(8,128)(2,1)S(1)}, bf16[64,384]{1,0:T(8,128)(2,1)S(1)}, u32[]{:S(2)}, u32[]{:S(2)}) collective-permute-start(bf16[64,384]{1,0:T(8,128)(2,1)S(1)} %shard_map.67.rows_ref), channel_id=1, source_target_pairs={{0,1},{1,3},{2,0},{3,2},{4,5},{5,7},{6,4},{7,6},{8,9},{9,11},{10,8... | collective-permute-start | bytes 147464 | tf_op jit(solution)/shard_map/ppermute | solution.py:254
  14.6 1.5 %collective-permute-start.12 = (bf16[64,384]{1,0:T(8,128)(2,1)S(1)}, bf16[64,384]{1,0:T(8,128)(2,1)S(1)}, u32[]{:S(2)}, u32[]{:S(2)}) collective-permute-start(bf16[64,384]{1,0:T(8,128)(2,1)S(1)} %shard_map.76.rows_ref), channel_id=1, source_target_pairs={{0,1},{1,3},{2,0},{3,2},{4,5},{5,7},{6,4},{7,6},{8,9},{9,11},{10,8... | collective-permute-start | bytes 147464 | tf_op jit(solution)/shard_map/ppermute | solution.py:254
  16.1 1.0 %collective-permute-done.4.partner_ref = bf16[64,384]{1,0:T(8,128)(2,1)S(1)} collective-permute-done((bf16[64,384]{1,0:T(8,128)(2,1)S(1)}, bf16[64,384]{1,0:T(8,128)(2,1)S(1)}, u32[]{:S(2)}, u32[]{:S(2)}) %collective-permute-start.4) | collective-permute-done | bytes 49184 | tf_op jit(solution)/shard_map/ppermute | solution.py:254
  17.1 1.6 %collective-permute-start.6 = (bf16[64,384]{1,0:T(8,128)(2,1)S(1)}, bf16[64,384]{1,0:T(8,128)(2,1)S(1)}, u32[]{:S(2)}, u32[]{:S(2)}) collective-permute-start(bf16[64,384]{1,0:T(8,128)(2,1)S(1)} %shard_map.69.rows_ref), channel_id=1, source_target_pairs={{0,1},{1,3},{2,0},{3,2},{4,5},{5,7},{6,4},{7,6},{8,9},{9,11},{10,8... | collective-permute-start | bytes 147464 | tf_op jit(solution)/shard_map/ppermute | solution.py:254
  18.7 1.5 %collective-permute-start.13 = (bf16[64,384]{1,0:T(8,128)(2,1)S(1)}, bf16[64,384]{1,0:T(8,128)(2,1)S(1)}, u32[]{:S(2)}, u32[]{:S(2)}) collective-permute-start(bf16[64,384]{1,0:T(8,128)(2,1)S(1)} %shard_map.77.rows_ref), channel_id=1, source_target_pairs={{0,1},{1,3},{2,0},{3,2},{4,5},{5,7},{6,4},{7,6},{8,9},{9,11},{10,8... | collective-permute-start | bytes 147464 | tf_op jit(solution)/shard_map/ppermute | solution.py:254
  20.2 1.0 %collective-permute-done.6.partner_ref = bf16[64,384]{1,0:T(8,128)(2,1)S(1)} collective-permute-done((bf16[64,384]{1,0:T(8,128)(2,1)S(1)}, bf16[64,384]{1,0:T(8,128)(2,1)S(1)}, u32[]{:S(2)}, u32[]{:S(2)}) %collective-permute-start.6) | collective-permute-done | bytes 49184 | tf_op jit(solution)/shard_map/ppermute | solution.py:254
  21.2 1.6 %collective-permute-start.8 = (bf16[64,384]{1,0:T(8,128)(2,1)S(1)}, bf16[64,384]{1,0:T(8,128)(2,1)S(1)}, u32[]{:S(2)}, u32[]{:S(2)}) collective-permute-start(bf16[64,384]{1,0:T(8,128)(2,1)S(1)} %shard_map.71.rows_ref), channel_id=1, source_target_pairs={{0,1},{1,3},{2,0},{3,2},{4,5},{5,7},{6,4},{7,6},{8,9},{9,11},{10,8... | collective-permute-start | bytes 147464 | tf_op jit(solution)/shard_map/ppermute | solution.py:254
  22.8 1.5 %collective-permute-start.14 = (bf16[64,384]{1,0:T(8,128)(2,1)S(1)}, bf16[64,384]{1,0:T(8,128)(2,1)S(1)}, u32[]{:S(2)}, u32[]{:S(2)}) collective-permute-start(bf16[64,384]{1,0:T(8,128)(2,1)S(1)} %shard_map.79.rows_ref), channel_id=1, source_target_pairs={{0,1},{1,3},{2,0},{3,2},{4,5},{5,7},{6,4},{7,6},{8,9},{9,11},{10,8... | collective-permute-start | bytes 147464 | tf_op jit(solution)/shard_map/ppermute | solution.py:254
  24.3 1.0 %collective-permute-done.8.partner_ref = bf16[64,384]{1,0:T(8,128)(2,1)S(1)} collective-permute-done((bf16[64,384]{1,0:T(8,128)(2,1)S(1)}, bf16[64,384]{1,0:T(8,128)(2,1)S(1)}, u32[]{:S(2)}, u32[]{:S(2)}) %collective-permute-start.8) | collective-permute-done | bytes 49184 | tf_op jit(solution)/shard_map/ppermute | solution.py:254
  25.3 1.6 %collective-permute-start.9 = (bf16[64,384]{1,0:T(8,128)(2,1)S(1)}, bf16[64,384]{1,0:T(8,128)(2,1)S(1)}, u32[]{:S(2)}, u32[]{:S(2)}) collective-permute-start(bf16[64,384]{1,0:T(8,128)(2,1)S(1)} %shard_map.72.rows_ref), channel_id=1, source_target_pairs={{0,1},{1,3},{2,0},{3,2},{4,5},{5,7},{6,4},{7,6},{8,9},{9,11},{10,8... | collective-permute-start | bytes 147464 | tf_op jit(solution)/shard_map/ppermute | solution.py:254
  26.9 1.9 %collective-permute-start.15 = (bf16[64,384]{1,0:T(8,128)(2,1)S(1)}, bf16[64,384]{1,0:T(8,128)(2,1)S(1)}, u32[]{:S(2)}, u32[]{:S(2)}) collective-permute-start(bf16[64,384]{1,0:T(8,128)(2,1)S(1)} %shard_map.80.rows_ref), channel_id=1, source_target_pairs={{0,1},{1,3},{2,0},{3,2},{4,5},{5,7},{6,4},{7,6},{8,9},{9,11},{10,8... | collective-permute-start | bytes 147464 | tf_op jit(solution)/shard_map/ppermute | solution.py:254
  29.4 1.6 %collective-permute-start.10 = (bf16[64,384]{1,0:T(8,128)(2,1)S(1)}, bf16[64,384]{1,0:T(8,128)(2,1)S(1)}, u32[]{:S(2)}, u32[]{:S(2)}) collective-permute-start(bf16[64,384]{1,0:T(8,128)(2,1)S(1)} %shard_map.73.rows_ref), channel_id=1, source_target_pairs={{0,1},{1,3},{2,0},{3,2},{4,5},{5,7},{6,4},{7,6},{8,9},{9,11},{10,8... | collective-permute-start | bytes 147464 | tf_op jit(solution)/shard_map/ppermute | solution.py:254
  31.0 1.9 %collective-permute-start.18 = (bf16[64,384]{1,0:T(8,128)(2,1)S(1)}, bf16[64,384]{1,0:T(8,128)(2,1)S(1)}, u32[]{:S(2)}, u32[]{:S(2)}) collective-permute-start(bf16[64,384]{1,0:T(8,128)(2,1)S(1)} %shard_map.81.rows_ref), channel_id=1, source_target_pairs={{0,1},{1,3},{2,0},{3,2},{4,5},{5,7},{6,4},{7,6},{8,9},{9,11},{10,8... | collective-permute-start | bytes 147464 | tf_op jit(solution)/shard_map/ppermute | solution.py:254
  32.9 0.7 %shard_map.82._ = bf16[128,384]{1,0:T(8,128)(2,1)} custom-call(bf16[64,384]{1,0:T(8,128)(2,1)S(1)} %collective-permute-done.16.first, bf16[64,384]{1,0:T(8,128)(2,1)S(1)} %collective-permute-done.17.second), custom_call_target="tpu_custom_call" | custom-call | bytes 196608 | tf_op jit(solution)/shard_map/pallas_call | solution.py:195
  33.6 1.4 %collective-permute-start.11 = (bf16[64,384]{1,0:T(8,128)(2,1)S(1)}, bf16[64,384]{1,0:T(8,128)(2,1)S(1)}, u32[]{:S(2)}, u32[]{:S(2)}) collective-permute-start(bf16[64,384]{1,0:T(8,128)(2,1)S(1)} %shard_map.74.rows_ref), channel_id=1, source_target_pairs={{0,1},{1,3},{2,0},{3,2},{4,5},{5,7},{6,4},{7,6},{8,9},{9,11},{10,8... | collective-permute-start | bytes 147464 | tf_op jit(solution)/shard_map/ppermute | solution.py:254
  35.1 1.9 %collective-permute-start.19 = (bf16[64,384]{1,0:T(8,128)(2,1)S(1)}, bf16[64,384]{1,0:T(8,128)(2,1)S(1)}, u32[]{:S(2)}, u32[]{:S(2)}) collective-permute-start(bf16[64,384]{1,0:T(8,128)(2,1)S(1)} %shard_map.83.rows_ref), channel_id=1, source_target_pairs={{0,1},{1,3},{2,0},{3,2},{4,5},{5,7},{6,4},{7,6},{8,9},{9,11},{10,8... | collective-permute-start | bytes 147464 | tf_op jit(solution)/shard_map/ppermute | solution.py:254
  37.0 0.8 %collective-permute-done.11.partner_ref = bf16[64,384]{1,0:T(8,128)(2,1)S(1)} collective-permute-done((bf16[64,384]{1,0:T(8,128)(2,1)S(1)}, bf16[64,384]{1,0:T(8,128)(2,1)S(1)}, u32[]{:S(2)}, u32[]{:S(2)}) %collective-permute-start.11) | collective-permute-done | bytes 49184 | tf_op jit(solution)/shard_map/ppermute | solution.py:254
  37.8 1.4 %collective-permute-done.19.partner_ref = bf16[64,384]{1,0:T(8,128)(2,1)S(1)} collective-permute-done((bf16[64,384]{1,0:T(8,128)(2,1)S(1)}, bf16[64,384]{1,0:T(8,128)(2,1)S(1)}, u32[]{:S(2)}, u32[]{:S(2)}) %collective-permute-start.19) | collective-permute-done | bytes 49184 | tf_op jit(solution)/shard_map/ppermute | solution.py:254
  (37 shorter events, 2.2 us)
Async XLA Ops:
  1.3 5.6 %collective-permute-start = (bf16[128,384]{1,0:T(8,128)(2,1)S(1)}, bf16[128,384]{1,0:T(8,128)(2,1)S(1)}, u32[]{:S(2)}, u32[]{:S(2)}) collective-permute-start(bf16[128,384]{1,0:T(8,128)(2,1)S(1)} %shard_map.64.rows_ref.x_ref), channel_id=1, source_target_pairs={{0,1},{1,0},{2,3},{3,2},{4,5},{5,4},{6,7},{7,6},{8,9},{9,8},{10,11... | collective-permute-start | bytes 294920 | tf_op jit(solution)/shard_map/ppermute | solution.py:254
  7.1 5.3 %collective-permute-start.3 = (bf16[2,384,384]{2,1,0:T(8,128)(2,1)S(1)}, bf16[2,384,384]{2,1,0:T(8,128)(2,1)S(1)}, u32[]{:S(2)}, u32[]{:S(2)}) collective-permute-start(bf16[2,384,384]{2,1,0:T(8,128)(2,1)S(1)} %get-tuple-element.37.table_ref), channel_id=1, source_target_pairs={{0,16},{1,17},{2,18},{3,19},{4,20},{5,21},{6,22},{7,23},{8,24},{9,... | collective-permute-start | bytes 1769480 | tf_op jit(solution)/shard_map/ppermute | solution.py:254
  7.2 5.2 %collective-permute-start.2 = (bf16[128,384]{1,0:T(8,128)(2,1)S(1)}, bf16[128,384]{1,0:T(8,128)(2,1)S(1)}, u32[]{:S(2)}, u32[]{:S(2)}) collective-permute-start(bf16[128,384]{1,0:T(8,128)(2,1)S(1)} %shard_map.66), channel_id=1, source_target_pairs={{0,18},{1,19},{2,16},{3,17},{4,22},{5,23},{6,20},{7,21},{8,26},{9,... | collective-permute-start | bytes 294920 | tf_op jit(solution)/shard_map/ppermute | solution.py:254
  9.4 3.1 %collective-permute-start.1 = (bf16[128,384]{1,0:T(8,128)(2,1)S(1)}, bf16[128,384]{1,0:T(8,128)(2,1)S(1)}, u32[]{:S(2)}, u32[]{:S(2)}) collective-permute-start(bf16[128,384]{1,0:T(8,128)(2,1)S(1)} %shard_map.66), channel_id=1, source_target_pairs={{0,16},{1,17},{2,18},{3,19},{4,20},{5,21},{6,22},{7,23},{8,24},{9,... | collective-permute-start | bytes 294920 | tf_op jit(solution)/shard_map/ppermute | solution.py:254
  12.4 4.7 %collective-permute-start.5 = (bf16[2,384,384]{2,1,0:T(8,128)(2,1)S(1)}, bf16[2,384,384]{2,1,0:T(8,128)(2,1)S(1)}, u32[]{:S(2)}, u32[]{:S(2)}) collective-permute-start(bf16[2,384,384]{2,1,0:T(8,128)(2,1)S(1)} %get-tuple-element.45.table_ref), channel_id=1, source_target_pairs={{0,16},{1,17},{2,18},{3,19},{4,20},{5,21},{6,22},{7,23},{8,24},{9,... | collective-permute-start | bytes 1769480 | tf_op jit(solution)/shard_map/ppermute | solution.py:254
  12.8 7.4 %collective-permute-start.7 = (bf16[2,384,384]{2,1,0:T(8,128)(2,1)S(1)}, bf16[2,384,384]{2,1,0:T(8,128)(2,1)S(1)}, u32[]{:S(2)}, u32[]{:S(2)}) collective-permute-start(bf16[2,384,384]{2,1,0:T(8,128)(2,1)S(1)} %get-tuple-element.46.table_ref), channel_id=1, source_target_pairs={{0,16},{1,17},{2,18},{3,19},{4,20},{5,21},{6,22},{7,23},{8,24},{9,... | collective-permute-start | bytes 1769480 | tf_op jit(solution)/shard_map/ppermute | solution.py:254
  13.0 4.1 %collective-permute-start.4 = (bf16[64,384]{1,0:T(8,128)(2,1)S(1)}, bf16[64,384]{1,0:T(8,128)(2,1)S(1)}, u32[]{:S(2)}, u32[]{:S(2)}) collective-permute-start(bf16[64,384]{1,0:T(8,128)(2,1)S(1)} %shard_map.67.rows_ref), channel_id=1, source_target_pairs={{0,1},{1,3},{2,0},{3,2},{4,5},{5,7},{6,4},{7,6},{8,9},{9,11},{10,8... | collective-permute-start | bytes 147464 | tf_op jit(solution)/shard_map/ppermute | solution.py:254
  14.6 4.1 %collective-permute-start.12 = (bf16[64,384]{1,0:T(8,128)(2,1)S(1)}, bf16[64,384]{1,0:T(8,128)(2,1)S(1)}, u32[]{:S(2)}, u32[]{:S(2)}) collective-permute-start(bf16[64,384]{1,0:T(8,128)(2,1)S(1)} %shard_map.76.rows_ref), channel_id=1, source_target_pairs={{0,1},{1,3},{2,0},{3,2},{4,5},{5,7},{6,4},{7,6},{8,9},{9,11},{10,8... | collective-permute-start | bytes 147464 | tf_op jit(solution)/shard_map/ppermute | solution.py:254
  17.1 4.1 %collective-permute-start.6 = (bf16[64,384]{1,0:T(8,128)(2,1)S(1)}, bf16[64,384]{1,0:T(8,128)(2,1)S(1)}, u32[]{:S(2)}, u32[]{:S(2)}) collective-permute-start(bf16[64,384]{1,0:T(8,128)(2,1)S(1)} %shard_map.69.rows_ref), channel_id=1, source_target_pairs={{0,1},{1,3},{2,0},{3,2},{4,5},{5,7},{6,4},{7,6},{8,9},{9,11},{10,8... | collective-permute-start | bytes 147464 | tf_op jit(solution)/shard_map/ppermute | solution.py:254
  18.7 4.1 %collective-permute-start.13 = (bf16[64,384]{1,0:T(8,128)(2,1)S(1)}, bf16[64,384]{1,0:T(8,128)(2,1)S(1)}, u32[]{:S(2)}, u32[]{:S(2)}) collective-permute-start(bf16[64,384]{1,0:T(8,128)(2,1)S(1)} %shard_map.77.rows_ref), channel_id=1, source_target_pairs={{0,1},{1,3},{2,0},{3,2},{4,5},{5,7},{6,4},{7,6},{8,9},{9,11},{10,8... | collective-permute-start | bytes 147464 | tf_op jit(solution)/shard_map/ppermute | solution.py:254
  21.2 4.1 %collective-permute-start.8 = (bf16[64,384]{1,0:T(8,128)(2,1)S(1)}, bf16[64,384]{1,0:T(8,128)(2,1)S(1)}, u32[]{:S(2)}, u32[]{:S(2)}) collective-permute-start(bf16[64,384]{1,0:T(8,128)(2,1)S(1)} %shard_map.71.rows_ref), channel_id=1, source_target_pairs={{0,1},{1,3},{2,0},{3,2},{4,5},{5,7},{6,4},{7,6},{8,9},{9,11},{10,8... | collective-permute-start | bytes 147464 | tf_op jit(solution)/shard_map/ppermute | solution.py:254
  22.8 4.1 %collective-permute-start.14 = (bf16[64,384]{1,0:T(8,128)(2,1)S(1)}, bf16[64,384]{1,0:T(8,128)(2,1)S(1)}, u32[]{:S(2)}, u32[]{:S(2)}) collective-permute-start(bf16[64,384]{1,0:T(8,128)(2,1)S(1)} %shard_map.79.rows_ref), channel_id=1, source_target_pairs={{0,1},{1,3},{2,0},{3,2},{4,5},{5,7},{6,4},{7,6},{8,9},{9,11},{10,8... | collective-permute-start | bytes 147464 | tf_op jit(solution)/shard_map/ppermute | solution.py:254
  25.3 4.1 %collective-permute-start.9 = (bf16[64,384]{1,0:T(8,128)(2,1)S(1)}, bf16[64,384]{1,0:T(8,128)(2,1)S(1)}, u32[]{:S(2)}, u32[]{:S(2)}) collective-permute-start(bf16[64,384]{1,0:T(8,128)(2,1)S(1)} %shard_map.72.rows_ref), channel_id=1, source_target_pairs={{0,1},{1,3},{2,0},{3,2},{4,5},{5,7},{6,4},{7,6},{8,9},{9,11},{10,8... | collective-permute-start | bytes 147464 | tf_op jit(solution)/shard_map/ppermute | solution.py:254
  26.9 4.1 %collective-permute-start.15 = (bf16[64,384]{1,0:T(8,128)(2,1)S(1)}, bf16[64,384]{1,0:T(8,128)(2,1)S(1)}, u32[]{:S(2)}, u32[]{:S(2)}) collective-permute-start(bf16[64,384]{1,0:T(8,128)(2,1)S(1)} %shard_map.80.rows_ref), channel_id=1, source_target_pairs={{0,1},{1,3},{2,0},{3,2},{4,5},{5,7},{6,4},{7,6},{8,9},{9,11},{10,8... | collective-permute-start | bytes 147464 | tf_op jit(solution)/shard_map/ppermute | solution.py:254
  28.8 4.1 %collective-permute-start.16 = (bf16[64,384]{1,0:T(8,128)(2,1)S(1)}, bf16[64,384]{1,0:T(8,128)(2,1)S(1)}, u32[]{:S(2)}, u32[]{:S(2)}) collective-permute-start(bf16[64,384]{1,0:T(8,128)(2,1)S(1)} %shard_map.70.front_ref), channel_id=1, source_target_pairs={{0,16},{1,17},{2,18},{3,19},{4,20},{5,21},{6,22},{7,23},{8,24},{9,... | collective-permute-start | bytes 147464 | tf_op jit(solution)/shard_map/ppermute | solution.py:254
  28.8 4.1 %collective-permute-start.17 = (bf16[64,384]{1,0:T(8,128)(2,1)S(1)}, bf16[64,384]{1,0:T(8,128)(2,1)S(1)}, u32[]{:S(2)}, u32[]{:S(2)}) collective-permute-start(bf16[64,384]{1,0:T(8,128)(2,1)S(1)} %shard_map.78.front_ref), channel_id=1, source_target_pairs={{0,16},{1,17},{2,18},{3,19},{4,20},{5,21},{6,22},{7,23},{8,24},{9,... | collective-permute-start | bytes 147464 | tf_op jit(solution)/shard_map/ppermute | solution.py:254
  29.4 4.2 %collective-permute-start.10 = (bf16[64,384]{1,0:T(8,128)(2,1)S(1)}, bf16[64,384]{1,0:T(8,128)(2,1)S(1)}, u32[]{:S(2)}, u32[]{:S(2)}) collective-permute-start(bf16[64,384]{1,0:T(8,128)(2,1)S(1)} %shard_map.73.rows_ref), channel_id=1, source_target_pairs={{0,1},{1,3},{2,0},{3,2},{4,5},{5,7},{6,4},{7,6},{8,9},{9,11},{10,8... | collective-permute-start | bytes 147464 | tf_op jit(solution)/shard_map/ppermute | solution.py:254
  31.0 4.1 %collective-permute-start.18 = (bf16[64,384]{1,0:T(8,128)(2,1)S(1)}, bf16[64,384]{1,0:T(8,128)(2,1)S(1)}, u32[]{:S(2)}, u32[]{:S(2)}) collective-permute-start(bf16[64,384]{1,0:T(8,128)(2,1)S(1)} %shard_map.81.rows_ref), channel_id=1, source_target_pairs={{0,1},{1,3},{2,0},{3,2},{4,5},{5,7},{6,4},{7,6},{8,9},{9,11},{10,8... | collective-permute-start | bytes 147464 | tf_op jit(solution)/shard_map/ppermute | solution.py:254
  33.6 4.1 %collective-permute-start.11 = (bf16[64,384]{1,0:T(8,128)(2,1)S(1)}, bf16[64,384]{1,0:T(8,128)(2,1)S(1)}, u32[]{:S(2)}, u32[]{:S(2)}) collective-permute-start(bf16[64,384]{1,0:T(8,128)(2,1)S(1)} %shard_map.74.rows_ref), channel_id=1, source_target_pairs={{0,1},{1,3},{2,0},{3,2},{4,5},{5,7},{6,4},{7,6},{8,9},{9,11},{10,8... | collective-permute-start | bytes 147464 | tf_op jit(solution)/shard_map/ppermute | solution.py:254
  35.1 4.1 %collective-permute-start.19 = (bf16[64,384]{1,0:T(8,128)(2,1)S(1)}, bf16[64,384]{1,0:T(8,128)(2,1)S(1)}, u32[]{:S(2)}, u32[]{:S(2)}) collective-permute-start(bf16[64,384]{1,0:T(8,128)(2,1)S(1)} %shard_map.83.rows_ref), channel_id=1, source_target_pairs={{0,1},{1,3},{2,0},{3,2},{4,5},{5,7},{6,4},{7,6},{8,9},{9,11},{10,8... | collective-permute-start | bytes 147464 | tf_op jit(solution)/shard_map/ppermute | solution.py:254
